TPU v7x, 32 devices: a whole 2x2x4 slice. The times are simulated.
32 devices in a mesh: grp: 2 (over x), orbit: 16 (over z, y, core).
Axes of the slice: x: 2, y: 2, z: 4, core: 2. Of those that a mesh axis runs over, the one named last changes fastest.
Arguments:
- solution: float32 [256, 8, 16, 128], P(('grp', 'orbit')), parts along dimension 0, may hold values from -6 to 6
- residual: float32 [256, 8, 16, 128], P(('grp', 'orbit')), parts along dimension 0, may hold values from -9 to 9
- direction: float32 [256, 8, 16, 128], P(('grp', 'orbit')), parts along dimension 0, may hold values from -9 to 9
- jacobian: bfloat16 [256, 24, 128, 128], P(('grp', 'orbit')), parts along dimension 0, may hold values from -0.109375 to 0.109375
- crossing: int32 [256, 24], P(('grp', 'orbit')), parts along dimension 0, may hold values from 0 to 127
- tile_count: int32 [32], P(('grp', 'orbit')), parts along dimension 0, may hold values from 1 to 8, as said below
- sightline_weight: float32 [256, 128], P(('grp', 'orbit')), parts along dimension 0, may hold values from 1 to 8
- length_class: int32 [256], P('grp'), parts along dimension 0, may hold values from 0 to 3
- smooth_weight: float32 [8, 128], replicated, may hold values from 0.2 to 2
Outputs:
- solution_next: float32 [256, 8, 16, 128], P(('grp', 'orbit')), parts along dimension 0
- residual_next: float32 [256, 8, 16, 128], P(('grp', 'orbit')), parts along dimension 0
- step_length: float32 [32], P('grp'), parts along dimension 0
There are 2 independent parts, one for each index of `grp`. A program takes and returns all parts, laid end to end along the dimension named above; an argument that names none is the same for every part. Nothing has to cross between parts.
Inputs may be any that keep to these rules, and one draw needn't show every extreme that they name: `tile_count`: slots at or above this count hold padding that carries no weight; in every draw some device has 8 live tiles. `crossing`: the window of a device starts 4 columns before its own block and covers 2 * 8 columns.
All inputs are finite; a program needn't handle non-finite values.
Results may differ from a plain program's by a relative error of at most 0.00075.
Values may be sent and summed in bfloat16 or wider, within the bound.
No kernel may reach another device: no remote copies, remote signals or barrier semaphores. Data moves between devices by JAX's collectives and lax.ppermute only.
A program may use at most 64 MiB of HBM per device.

v0:
```python
import functools

import jax
import jax.numpy as jnp
from jax import lax
from jax.experimental import pallas as pl
from jax.experimental.pallas import tpu as pltpu
from jax.sharding import PartitionSpec as P

LEVELS = 120
CLASSES = 4
REACH = 8
EPSILON = 1e-06
GROUP = 2
VMEM_LIMIT = 24 * 1024 * 1024

SMEM = functools.partial(pl.BlockSpec, memory_space=pltpu.SMEM)
VMEM = functools.partial(pl.BlockSpec, memory_space=pltpu.VMEM)
HBM = functools.partial(pl.BlockSpec, memory_space=pltpu.HBM)


def in_hbm(array):
    return pltpu.with_memory_space_constraint(array, pltpu.HBM)


def live_lanes(shape):
    return lax.broadcasted_iota(jnp.int32, shape, len(shape) - 1) < LEVELS


def masked(values):
    return jnp.where(live_lanes(values.shape), values, 0.0)


def call(kernel, out_shape, in_specs, flops, moved, scratch=(), out_specs=None):
    return pl.pallas_call(
        kernel,
        out_shape=out_shape,
        in_specs=in_specs,
        out_specs=tuple(out_specs or [VMEM()] * len(out_shape)),
        scratch_shapes=list(scratch),
        compiler_params=pltpu.CompilerParams(vmem_limit_bytes=VMEM_LIMIT),
        cost_estimate=pl.CostEstimate(flops=flops, bytes_accessed=moved, transcendentals=0),
    )


def parity():
    return lax.rem(lax.axis_index("orbit"), 2)


def rounding_kernel(direction_hbm, direction, across, within, sems):
    rim = across.shape[0]
    odd = parity()
    halves = ((odd, across), (1 - odd, within))
    copies = []
    for k, (place, _) in enumerate(halves):
        half = pl.ds(place * rim, rim)
        copies.append(
            pltpu.make_async_copy(direction_hbm.at[half], direction.at[half], sems.at[k])
        )
        copies[-1].start()
    for copy, (place, half) in zip(copies, halves):
        copy.wait()
        for c in range(rim):
            half[c] = masked(direction[place * rim + c]).astype(jnp.bfloat16)


def coupling(classes, cols, columns):
    total = classes.shape[0]
    first = lax.axis_index("orbit") * cols
    table = {}
    for c in columns:
        length = (classes[lax.rem(first + c + total, total)] + 1) * REACH // CLASSES
        for k in range(1, REACH + 1):
            table[c, k] = jnp.where(k <= length, jnp.float32(1.0 / (k * k)), jnp.float32(0.0))
    return table


def pull(table, to, values):
    result = None
    for c, value in values.items():
        if c != to and abs(c - to) <= REACH:
            term = table[min(c, to), abs(c - to)] * value
            result = term if result is None else result + term
    return 0.0 if result is None else -result


def slot_groups(slots):
    return [range(i, min(i + GROUP, slots)) for i in range(0, slots, GROUP)]


def if_live(count, group, work):
    if group[0] == 0:
        work()
    else:
        pl.when(group[0] < count)(work)


def inner_kernel(
    direction, count, residual_hbm, classes_hbm, smooth_hbm, sight_hbm, crossing_hbm, jac_hbm,
    begun, faced, norm, curved, rows, jac, crossing, classes, live, residual, smooth, sight, sems,
):
    pairs = (
        (classes_hbm, classes), (smooth_hbm, smooth), (sight_hbm, sight),
        (residual_hbm, residual), (crossing_hbm, crossing),
    )
    copies = [pltpu.make_async_copy(*pair, sems.at[i]) for i, pair in enumerate(pairs)]
    for copy in copies:
        copy.start()

    def load(group):
        part = pl.ds(group[0], len(group))
        return pltpu.make_async_copy(
            jac_hbm.at[part], jac.at[part], sems.at[len(pairs) + group[0] // GROUP]
        )

    for group in slot_groups(jac.shape[0]):
        if_live(count[0], group, lambda: load(group).start())
    live[0] = count[0]
    copies[0].wait()
    copies[1].wait()
    cols = direction.shape[0]
    rim = cols // 2
    table = coupling(classes, cols, range(-REACH, cols))
    weight = smooth[...][:, None, :]
    total = jnp.zeros(norm.shape, jnp.float32)
    values = {c: masked(direction[c]) for c in range(cols)}
    rests = {c: v - v.astype(jnp.bfloat16).astype(jnp.float32) for c, v in values.items()}
    for c in range(cols):
        centre = jnp.float32(1.0)
        for k in range(1, REACH + 1):
            centre = centre + (table[c, k] + table[c - k, k])
        result = weight * (centre * values[c] + pull(table, c, values))
        begun[rim + c] = result
        total = total + jnp.sum(values[c] * result, axis=0)
    low = {c: values[c] for c in range(rim)}
    high = {c: values[c] for c in range(rim, cols)}
    low_rests = {c: rests[c] for c in range(rim)}
    high_rests = {c: rests[c] for c in range(rim, cols)}
    for q in range(rim):
        facing = weight * pull(table, q - rim, high)
        faced[0, q] = facing
        begun[q] = facing + weight * pull(table, q - rim, low_rests)
        facing = weight * pull(table, q + cols, low)
        faced[1, q] = facing + weight * pull(table, q + cols, high)
        begun[rim + cols + q] = facing + weight * pull(table, q + cols, high_rests)
    curved[...] = total
    copies[2].wait()
    slot = lax.broadcasted_iota(jnp.int32, rows.shape, 0)
    rows[...] = jnp.where(slot < count[0], sight[...], 0.0)
    copies[3].wait()
    squares = jnp.zeros(norm.shape, jnp.float32)
    for c in range(cols):
        mres = masked(residual[c])
        squares = squares + jnp.sum(mres * mres, axis=0)
    norm[...] = squares
    copies[4].wait()
    for group in slot_groups(jac.shape[0]):
        if_live(count[0], group, lambda: load(group).wait())


def forward_kernel(
    crossing, live, rows, across, within, from_across, from_within, faced, norm, curved, jac,
    weighted, sums, window, total,
):
    slots, crossings = crossing.shape
    rim, species = across.shape[:2]
    span = rim * species
    odd = parity()
    places = (1 + odd, across), (2 - odd, within), (3 * odd, from_across), (3 - 3 * odd, from_within)
    for place, part in places:
        window[pl.ds(place * span, span)] = part[...].reshape(span, *part.shape[2:])
    edges = curved[...]
    for q in range(rim):
        for side, part in (odd, from_across), (1 - odd, from_within):
            edges = edges + 2.0 * jnp.sum(faced[side, q] * part[q].astype(jnp.float32), axis=0)
    total[...] = edges

    def project(group):
        added = jnp.zeros(total.shape, jnp.float32)
        for i in group:
            picked = jnp.concatenate([window[crossing[i, j]] for j in range(crossings)], axis=1)
            tiles = jnp.concatenate([jac[i, j] for j in range(crossings)], axis=1)
            integrals = lax.dot_general(
                picked, tiles, (((1,), (1,)), ((), ())), preferred_element_type=jnp.float32
            )
            product = (rows[pl.ds(i, 1), :] * integrals).astype(jnp.bfloat16)
            weighted[i] = product
            added = added + product.astype(jnp.float32) * integrals
        total[...] += added

    for group in slot_groups(slots):
        if_live(live[0], group, lambda: project(group))
    half = sums.shape[0]
    parts = [jnp.sum(x, axis=1, keepdims=True) for x in (norm[...], total[...])]
    parts = [part[h * half : (h + 1) * half] for h in range(2) for part in parts]
    lane = lax.broadcasted_iota(jnp.int32, sums.shape, 1)
    block = jnp.zeros(sums.shape, jnp.float32)
    for k, part in enumerate(parts):
        block = jnp.where(lane == k, part, block)
    sums[...] = block


def backward_kernel(
    crossing, classes, live, smooth, weighted, jac, begun, from_across, from_within,
    image, across, within, sums, near,
):
    slots, crossings = crossing.shape
    cols, species, probes, tile = image.shape
    rim = across.shape[0]
    span = rim * species
    odd = parity()
    near[odd] = from_across[...].astype(jnp.float32)
    near[1 - odd] = from_within[...].astype(jnp.float32)
    table = coupling(classes, cols, range(-rim, cols))
    weight = smooth[...][:, None, :]
    beside = {q - rim: near[0, q] for q in range(rim)} | {q + cols: near[1, q] for q in range(rim)}
    for c in range(cols):
        place = pl.ds(span + c * species, species)
        sums[place] = begun[rim + c] + weight * pull(table, c, beside)
    sums[pl.ds(0, span)] = begun[pl.ds(0, rim)].reshape(span, probes, tile)
    sums[pl.ds(3 * span, span)] = begun[pl.ds(rim + cols, rim)].reshape(span, probes, tile)

    def project(group):
        for i in group:
            tiles = jnp.concatenate([jac[i, j] for j in range(crossings)], axis=1)
            terms = jnp.dot(weighted[i], tiles, preferred_element_type=jnp.float32)
            for j in range(crossings):
                sums[crossing[i, j]] += terms[:, j * tile : (j + 1) * tile]

    for group in slot_groups(slots):
        if_live(live[0], group, lambda: project(group))
    for part, place in (across, 3 * odd), (within, 3 - 3 * odd):
        part[...] = sums[pl.ds(place * span, span)].astype(part.dtype).reshape(part.shape)
    image[...] = sums[pl.ds(span, 2 * span)].reshape(image.shape)


def final_kernel(
    solution, residual, direction, image, from_across, from_within, *rest
):
    *held, solution_next, residual_next, step_length = rest
    whole = tree_sum([part[...] for part in held])
    norm = jnp.concatenate([whole[:, 0:1], whole[:, 2:3]], axis=0)
    curvature = jnp.concatenate([whole[:, 1:2], whole[:, 3:4]], axis=0)
    step = norm / (curvature + EPSILON)
    rim = from_across.shape[0]
    wide = jnp.broadcast_to(step, direction.shape[2:])
    step_length[...] = jnp.transpose(wide)[0:1]
    wide = wide[None]
    odd = parity()
    for q in range(rim):
        for c, part in (odd * rim + q, from_across), ((1 - odd) * rim + q, from_within):
            total = masked(image[c] + part[q].astype(jnp.float32))
            solution_next[c] = masked(solution[c] + wide * direction[c])
            residual_next[c] = masked(residual[c]) - wide * total


def swapped_across(half):
    count = lax.axis_size("orbit")
    assert count % 2 == 0
    return lax.ppermute(half, "orbit", [(i, (i + 2 * (i % 2) - 1) % count) for i in range(count)])


def swapped_within(half):
    return lax.ppermute(half, "orbit", [(i, i ^ 1) for i in range(lax.axis_size("orbit"))])


def sum_steps(devices):
    assert devices >= 8 and devices & (devices - 1) == 0
    return [[1 << b] for b in range(1, devices.bit_length() - 2)] + [[1, devices // 2]]


def partners(array, bits):
    devices = range(lax.axis_size("orbit"))
    masks = [sum(bit for k, bit in enumerate(bits) if m >> k & 1) for m in range(1, 1 << len(bits))]
    found = {
        mask: lax.ppermute(array, "orbit", [(i, i ^ mask) for i in devices]) for mask in masks[::-1]
    }
    return [found[mask] for mask in masks]


def tree_sum(parts):
    while len(parts) > 1:
        parts = [parts[k] + parts[k + 1] for k in range(0, len(parts), 2)]
    return parts[0]


def local(
    solution, residual, direction, jacobian, crossing, tile_count, sightline_weight,
    length_class, smooth_weight,
):
    cols, species, probes, width = direction.shape
    assert REACH <= cols
    rim = cols // 2
    slots = crossing.shape[0]
    f32, bf16 = jnp.float32, jnp.bfloat16
    shape = jax.ShapeDtypeStruct
    column = (species, probes, width)
    elements = direction.size
    dot_flops = 2 * jacobian.size * probes
    near = shape((rim,) + column, bf16)
    whole = shape(direction.shape, f32)
    small = shape((probes, width), f32)

    held, across, within = call(
        rounding_kernel,
        (whole, near, near),
        [HBM()],
        2 * elements,
        10 * elements,
        [pltpu.SemaphoreType.DMA((2,))],
    )(in_hbm(direction))
    from_across, from_within = swapped_across(across), swapped_within(within)

    begun, faced, norm, curved, rows, jac, crossing, length_class, live = call(
        inner_kernel,
        (
            shape((2 * cols,) + column, f32), shape((2, rim) + column, f32), small, small,
            shape(sightline_weight.shape, f32), shape(jacobian.shape, bf16),
            pltpu.SMEM(crossing.shape, jnp.int32), pltpu.SMEM(length_class.shape, jnp.int32),
            pltpu.SMEM((8,), jnp.int32),
        ),
        [VMEM(), SMEM()] + [HBM()] * 6,
        60 * elements,
        4 * jacobian.size,
        [
            pltpu.VMEM(direction.shape, f32),
            pltpu.VMEM(smooth_weight.shape, f32),
            pltpu.VMEM(sightline_weight.shape, f32),
            pltpu.SemaphoreType.DMA((5 + len(slot_groups(slots)),)),
        ],
        [VMEM()] * 6 + [SMEM()] * 3,
    )(
        held, tile_count,
        *map(in_hbm, (
            residual, length_class, smooth_weight, sightline_weight, crossing, jacobian,
        )),
    )

    devices = lax.axis_size("orbit")
    peers = devices // 2
    weighted, sums = call(
        forward_kernel,
        (shape((slots, probes, width), bf16), shape((probes // 2, width), f32)),
        [SMEM()] * 2 + [VMEM()] * 9,
        dot_flops,
        2 * jacobian.size,
        [pltpu.VMEM((2 * cols * species, probes, width), bf16), pltpu.VMEM((probes, width), f32)],
    )(crossing, live, rows, across, within, from_across, from_within, faced, norm, curved, jac)
    near_step, *far_steps = sum_steps(devices)
    held = [sums] + partners(sums, near_step)

    image, across, within = call(
        backward_kernel,
        (whole, near, near),
        [SMEM()] * 3 + [VMEM()] * 6,
        dot_flops,
        2 * jacobian.size,
        [
            pltpu.VMEM((2 * cols * species, probes, width), f32),
            pltpu.VMEM((2, rim) + column, f32),
        ],
    )(crossing, length_class, live, smooth_weight, weighted, jac, begun, from_across, from_within)
    from_across = swapped_across(across)
    within, *held = lax.optimization_barrier((within, *held))
    sums = tree_sum(held)
    held = [sums] + partners(sums, far_steps[0])
    within, *held = lax.optimization_barrier((within, *held))
    from_within = swapped_within(within)
    for step in far_steps[1:]:
        sums = tree_sum(held)
        held = [sums] + partners(sums, step)

    solution_next, residual_next, step_length = call(
        final_kernel,
        (whole, whole, shape((1, probes), f32)),
        [VMEM()] * (6 + len(held)),
        8 * elements,
        28 * elements,
    )(solution, residual, direction, image, from_across, from_within, *held)
    return solution_next, residual_next, step_length.reshape(probes)


def solution(mesh):
    wide = P(("grp", "orbit"), None, None, None)
    placed = (
        wide, wide, wide, wide,
        P(("grp", "orbit"), None),
        P(("grp", "orbit")),
        P(("grp", "orbit"), None),
        P("grp"),
        P(),
    )
    return jax.shard_map(
        local, mesh=mesh, in_specs=placed, out_specs=(wide, wide, P("grp")), check_vma=False
    )
```

profile of v0, /device:TPU:0, one launch (start us, length us, event | category | flops | bytes accessed | tf_op | source)
XLA Modules:
  0.0 26.8 jit_solution(9191575845657804284)
XLA Ops:
  0.6 1.1 %shard_map.112 = (f32[8,8,16,128]{3,2,1,0:T(8,128)S(1)}, bf16[4,8,16,128]{3,2,1,0:T(8,128)(2,1)S(1)}, bf16[4,8,16,128]{3,2,1,0:T(8,128)(2,1)S(1)}) custom-call(f32[8,8,16,128]{3,2,1,0:T(8,128)} %direction.1), custom_call_target="tpu_custom_call" | custom-call | flops 262144 | bytes 1310720 | tf_op jit(solution)/shard_map/pallas_call | solution.py:304
  1.7 5.5 %collective-permute-start = (bf16[4,8,16,128]{3,2,1,0:T(8,128)(2,1)S(1)}, bf16[4,8,16,128]{3,2,1,0:T(8,128)(2,1)S(1)}, u32[]{:S(2)}, u32[]{:S(2)}) collective-permute-start(bf16[4,8,16,128]{3,2,1,0:T(8,128)(2,1)S(1)} %get-tuple-element.34.across), channel_id=1, source_target_pairs={{0,15},{1,2},{2,1},{3,4},{4,3},{5,6},{6,5},{7,8},{8,7},{9,10},{10,... | collective-permute-start | bytes 393224 | tf_op jit(solution)/shard_map/ppermute | solution.py:260
  7.2 0.0 collective-permute-start.1
  7.9 0.0 copy-start.3
  7.9 3.1 %shard_map.113 = (f32[16,8,16,128]{3,2,1,0:T(8,128)S(1)}, f32[2,4,8,16,128]{4,3,2,1,0:T(8,128)S(1)}, f32[16,128]{1,0:T(8,128)S(1)}, f32[16,128]{1,0:T(8,128)S(1)...) custom-call(f32[8,8,16,128]{3,2,1,0:T(8,128)S(1)} %get-tuple-element, ...), custom_call_target="tpu_custom_call" | custom-call | flops 7864320 | bytes 12582912 | tf_op jit(solution)/shard_map/pallas_call | solution.py:314
  11.0 0.0 collective-permute-done.from_across
  11.0 0.0 collective-permute-done.1.from_within
  11.0 0.0 copy-start
  11.0 0.0 copy-start.1
  11.1 0.0 copy-start.2
  11.1 2.2 %shard_map.114 = (bf16[8,16,128]{2,1,0:T(8,128)(2,1)S(1)}, f32[8,128]{1,0:T(8,128)S(1)}) custom-call(s32[8,24]{1,0:T(8,128)S(4)} %get-tuple-element.30.crossing, s32[8]{0:T(128)S(4)} %get-tuple-element.32.live, f32[8,128]{1,0:T(8,128)S(1)} %get-tuple-element.33.rows, bf16[4,8,16,128]{3,2,1,0:T(8,128)(2,1)S(1)} %get-tuple-element.34.across, ...), custom_call_target="tpu_custom_call" | custom-call | flops 100663296 | bytes 6291456 | tf_op jit(solution)/shard_map/pallas_call | solution.py:341
  13.2 0.0 collective-permute-start.3
  13.3 0.0 copy-done.3
  13.3 1.8 %shard_map.115 = (f32[8,8,16,128]{3,2,1,0:T(8,128)S(1)}, bf16[4,8,16,128]{3,2,1,0:T(8,128)(2,1)S(1)}, bf16[4,8,16,128]{3,2,1,0:T(8,128)(2,1)S(1)}) custom-call(s32[8,24]{1,0:T(8,128)S(4)} %get-tuple-element.30.crossing, s32[128]{0:T(128)S(4)} %get-tuple-element.31.classes, s32[8]{0:T(128)S(4)} %get-tuple-element.32.live, f32[8,128]{1,0:T(8,128)S(1)} %copy-done.3, ...), custom_call_target="tpu_custom_call" | custom-call | flops 100663296 | bytes 6291456 | tf_op jit(solution)/shard_map/pallas_call | solution.py:352
  15.1 1.8 %collective-permute-done.3 = f32[8,128]{1,0:T(8,128)S(1)} collective-permute-done((f32[8,128]{1,0:T(8,128)S(1)}, f32[8,128]{1,0:T(8,128)S(1)}, u32[]{:S(2)}, u32[]{:S(2)}) %collective-permute-start.3) | collective-permute-done | bytes 4128 | tf_op jit(solution)/shard_map/ppermute | solution.py:276
  16.9 0.0 collective-permute-start.4
  16.9 2.1 %collective-permute-start.2 = (bf16[4,8,16,128]{3,2,1,0:T(8,128)(2,1)S(1)}, bf16[4,8,16,128]{3,2,1,0:T(8,128)(2,1)S(1)}, u32[]{:S(2)}, u32[]{:S(2)}) collective-permute-start(bf16[4,8,16,128]{3,2,1,0:T(8,128)(2,1)S(1)} %get-tuple-element.43), channel_id=1, source_target_pairs={{0,15},{1,2},{2,1},{3,4},{4,3},{5,6},{6,5},{7,8},{8,7},{9,10},{10,... | collective-permute-start | bytes 393224 | tf_op jit(solution)/shard_map/ppermute | solution.py:260
  19.0 1.5 %collective-permute-done.4 = f32[8,128]{1,0:T(8,128)S(1)} collective-permute-done((f32[8,128]{1,0:T(8,128)S(1)}, f32[8,128]{1,0:T(8,128)S(1)}, u32[]{:S(2)}, u32[]{:S(2)}) %collective-permute-start.4) | collective-permute-done | bytes 4128 | tf_op jit(solution)/shard_map/ppermute | solution.py:276
  20.5 0.0 collective-permute-start.5
  20.5 0.5 %collective-permute-start.6 = (f32[8,128]{1,0:T(8,128)S(1)}, f32[8,128]{1,0:T(8,128)S(1)}, u32[]{:S(2)}, u32[]{:S(2)}) collective-permute-start(f32[8,128]{1,0:T(8,128)S(1)} %add.7.rest_0_), channel_id=1, source_target_pairs={{0,1},{1,0},{2,3},{3,2},{4,5},{5,4},{6,7},{7,6},{8,9},{9,8},{10,11... | collective-permute-start | bytes 12296 | tf_op jit(solution)/shard_map/ppermute | solution.py:276
  21.0 0.2 collective-permute-start.7
  21.2 2.0 %collective-permute-start.8 = (f32[8,128]{1,0:T(8,128)S(1)}, f32[8,128]{1,0:T(8,128)S(1)}, u32[]{:S(2)}, u32[]{:S(2)}) collective-permute-start(f32[8,128]{1,0:T(8,128)S(1)} %add.7.rest_0_), channel_id=1, source_target_pairs={{0,9},{1,8},{2,11},{3,10},{4,13},{5,12},{6,15},{7,14},{8,1},{9,0},... | collective-permute-start | bytes 12296 | tf_op jit(solution)/shard_map/ppermute | solution.py:276
  23.2 0.0 collective-permute-done.6.rest_1_
  23.2 2.2 %collective-permute-done.7.rest_2_ = f32[8,128]{1,0:T(8,128)S(1)} collective-permute-done((f32[8,128]{1,0:T(8,128)S(1)}, f32[8,128]{1,0:T(8,128)S(1)}, u32[]{:S(2)}, u32[]{:S(2)}) %collective-permute-start.7) | collective-permute-done | bytes 4128 | tf_op jit(solution)/shard_map/ppermute | solution.py:276
  25.5 0.0 collective-permute-done.8.rest_3_
  25.5 0.0 collective-permute-done.2.from_across
  25.5 0.0 collective-permute-done.5.from_within
  25.5 0.0 copy-done
  25.5 0.0 copy-done.1
  25.5 0.0 copy-done.2
  25.5 1.2 %shard_map.116 = (f32[8,8,16,128]{3,2,1,0:T(8,128)}, f32[8,8,16,128]{3,2,1,0:T(8,128)}, f32[1,16]{1,0:T(1,128)}) custom-call(f32[8,8,16,128]{3,2,1,0:T(8,128)S(1)} %copy-done.2, f32[8,8,16,128]{3,2,1,0:T(8,128)S(1)} %copy-done.1, f32[8,8,16,128]{3,2,1,0:T(8,128)S(1)} %copy-done, f32[8,8,16,128]{3,2,1,0:T(8,128)S(1)} %get-tuple-element.42.image, ...), custom_call_target="tpu_custom_call" | custom-call | flops 1048576 | bytes 3670016 | tf_op jit(solution)/shard_map/pallas_call | solution.py:373
  (2 shorter events, 0.0 us)
Async XLA Ops:
  1.7 9.3 %collective-permute-start = (bf16[4,8,16,128]{3,2,1,0:T(8,128)(2,1)S(1)}, bf16[4,8,16,128]{3,2,1,0:T(8,128)(2,1)S(1)}, u32[]{:S(2)}, u32[]{:S(2)}) collective-permute-start(bf16[4,8,16,128]{3,2,1,0:T(8,128)(2,1)S(1)} %get-tuple-element.34.across), channel_id=1, source_target_pairs={{0,15},{1,2},{2,1},{3,4},{4,3},{5,6},{6,5},{7,8},{8,7},{9,10},{10,... | collective-permute-start | bytes 393224 | tf_op jit(solution)/shard_map/ppermute | solution.py:260
  7.2 3.8 %collective-permute-start.1 = (bf16[4,8,16,128]{3,2,1,0:T(8,128)(2,1)S(1)}, bf16[4,8,16,128]{3,2,1,0:T(8,128)(2,1)S(1)}, u32[]{:S(2)}, u32[]{:S(2)}) collective-permute-start(bf16[4,8,16,128]{3,2,1,0:T(8,128)(2,1)S(1)} %get-tuple-element.35.within), channel_id=1, source_target_pairs={{0,1},{1,0},{2,3},{3,2},{4,5},{5,4},{6,7},{7,6},{8,9},{9,8},{10,11... | collective-permute-start | bytes 393224 | tf_op jit(solution)/shard_map/ppermute | solution.py:264
  7.9 5.4 %copy-start.3 = (f32[8,128]{1,0:T(8,128)S(1)}, f32[8,128]{1,0:T(8,128)}, u32[]{:S(2)}) copy-start(f32[8,128]{1,0:T(8,128)} %smooth.1) | copy-start | bytes 12292
  11.0 14.5 %copy-start = (f32[8,8,16,128]{3,2,1,0:T(8,128)S(1)}, f32[8,8,16,128]{3,2,1,0:T(8,128)}, u32[]{:S(2)}) copy-start(f32[8,8,16,128]{3,2,1,0:T(8,128)} %direction.1) | copy-start | bytes 1572868
  11.0 14.5 %copy-start.1 = (f32[8,8,16,128]{3,2,1,0:T(8,128)S(1)}, f32[8,8,16,128]{3,2,1,0:T(8,128)}, u32[]{:S(2)}) copy-start(f32[8,8,16,128]{3,2,1,0:T(8,128)} %residual.1) | copy-start | bytes 1572868
  11.1 14.5 %copy-start.2 = (f32[8,8,16,128]{3,2,1,0:T(8,128)S(1)}, f32[8,8,16,128]{3,2,1,0:T(8,128)}, u32[]{:S(2)}) copy-start(f32[8,8,16,128]{3,2,1,0:T(8,128)} %solution.1) | copy-start | bytes 1572868
  13.2 3.6 %collective-permute-start.3 = (f32[8,128]{1,0:T(8,128)S(1)}, f32[8,128]{1,0:T(8,128)S(1)}, u32[]{:S(2)}, u32[]{:S(2)}) collective-permute-start(f32[8,128]{1,0:T(8,128)S(1)} %get-tuple-element.47), channel_id=1, source_target_pairs={{0,2},{1,3},{2,0},{3,1},{4,6},{5,7},{6,4},{7,5},{8,10},{9,11},{10,... | collective-permute-start | bytes 12296 | tf_op jit(solution)/shard_map/ppermute | solution.py:276
  16.9 3.6 %collective-permute-start.4 = (f32[8,128]{1,0:T(8,128)S(1)}, f32[8,128]{1,0:T(8,128)S(1)}, u32[]{:S(2)}, u32[]{:S(2)}) collective-permute-start(f32[8,128]{1,0:T(8,128)S(1)} %add.6), channel_id=1, source_target_pairs={{0,4},{1,5},{2,6},{3,7},{4,0},{5,1},{6,2},{7,3},{8,12},{9,13},{10,... | collective-permute-start | bytes 12296 | tf_op jit(solution)/shard_map/ppermute | solution.py:276
  16.9 8.6 %collective-permute-start.2 = (bf16[4,8,16,128]{3,2,1,0:T(8,128)(2,1)S(1)}, bf16[4,8,16,128]{3,2,1,0:T(8,128)(2,1)S(1)}, u32[]{:S(2)}, u32[]{:S(2)}) collective-permute-start(bf16[4,8,16,128]{3,2,1,0:T(8,128)(2,1)S(1)} %get-tuple-element.43), channel_id=1, source_target_pairs={{0,15},{1,2},{2,1},{3,4},{4,3},{5,6},{6,5},{7,8},{8,7},{9,10},{10,... | collective-permute-start | bytes 393224 | tf_op jit(solution)/shard_map/ppermute | solution.py:260
  20.5 5.0 %collective-permute-start.5 = (bf16[4,8,16,128]{3,2,1,0:T(8,128)(2,1)S(1)}, bf16[4,8,16,128]{3,2,1,0:T(8,128)(2,1)S(1)}, u32[]{:S(2)}, u32[]{:S(2)}) collective-permute-start(bf16[4,8,16,128]{3,2,1,0:T(8,128)(2,1)S(1)} %get-tuple-element.49), channel_id=1, source_target_pairs={{0,1},{1,0},{2,3},{3,2},{4,5},{5,4},{6,7},{7,6},{8,9},{9,8},{10,11... | collective-permute-start | bytes 393224 | tf_op jit(solution)/shard_map/ppermute | solution.py:264
  20.5 2.8 %collective-permute-start.6 = (f32[8,128]{1,0:T(8,128)S(1)}, f32[8,128]{1,0:T(8,128)S(1)}, u32[]{:S(2)}, u32[]{:S(2)}) collective-permute-start(f32[8,128]{1,0:T(8,128)S(1)} %add.7.rest_0_), channel_id=1, source_target_pairs={{0,1},{1,0},{2,3},{3,2},{4,5},{5,4},{6,7},{7,6},{8,9},{9,8},{10,11... | collective-permute-start | bytes 12296 | tf_op jit(solution)/shard_map/ppermute | solution.py:276
  21.0 4.5 %collective-permute-start.7 = (f32[8,128]{1,0:T(8,128)S(1)}, f32[8,128]{1,0:T(8,128)S(1)}, u32[]{:S(2)}, u32[]{:S(2)}) collective-permute-start(f32[8,128]{1,0:T(8,128)S(1)} %add.7.rest_0_), channel_id=1, source_target_pairs={{0,8},{1,9},{2,10},{3,11},{4,12},{5,13},{6,14},{7,15},{8,0},{9,1},... | collective-permute-start | bytes 12296 | tf_op jit(solution)/shard_map/ppermute | solution.py:276
  21.2 4.3 %collective-permute-start.8 = (f32[8,128]{1,0:T(8,128)S(1)}, f32[8,128]{1,0:T(8,128)S(1)}, u32[]{:S(2)}, u32[]{:S(2)}) collective-permute-start(f32[8,128]{1,0:T(8,128)S(1)} %add.7.rest_0_), channel_id=1, source_target_pairs={{0,9},{1,8},{2,11},{3,10},{4,13},{5,12},{6,15},{7,14},{8,1},{9,0},... | collective-permute-start | bytes 12296 | tf_op jit(solution)/shard_map/ppermute | solution.py:276
where the time goes:
time: 26.5 us; the launch traced here: 26.8 us
  starting transfers between devices  10.4 us (39%)
  Pallas kernels  9.39 us (35%)
  waiting for transfers between devices  5.55 us (21%)
  between operations  1.4 us (5%)
    ppermute x2, starting transfers between devices, swapped_across(): lax.ppermute(half, 'orbit', [(i, (i + 2 * (i % 2) - 1) % count) for i in...  7.63 us
    ppermute x5, waiting for transfers between devices, partners(): lax.ppermute(array, 'orbit', [(i, i ^ mask) for i in devices])  5.54 us
    pallas_call x1, Pallas kernels, local(): call(inner_kernel, (shape((2 * cols,) + column, f32), shape((2, rim) + co...  3.11 us
    ppermute x5, starting transfers between devices, partners(): lax.ppermute(array, 'orbit', [(i, i ^ mask) for i in devices])  2.77 us
    pallas_call x1, Pallas kernels, local(): call(forward_kernel, (shape((slots, probes, width), bf16), shape((probes...  2.18 us
    pallas_call x1, Pallas kernels, local(): call(backward_kernel, (whole, near, near), [SMEM()] * 3 + [VMEM()] * 6, d...  1.79 us
    pallas_call x1, Pallas kernels, local(): call(final_kernel, (whole, whole, shape((1, probes), f32)), [VMEM()] * (6...  1.24 us
    pallas_call x1, Pallas kernels, local(): call(rounding_kernel, (whole, near, near), [HBM()], 2 * elements, 10 * el...  1.07 us
  transfers between devices with their start and end apart: 9, of which 3 were waited for; matrix products, arithmetic and copies ran while one was open for 0% of the time, Pallas kernels for 18%

commit v1 on v0

--- a/solution.py
+++ b/solution.py
@@ -275,7 +275,7 @@
     found = {
         mask: lax.ppermute(array, "orbit", [(i, i ^ mask) for i in devices]) for mask in masks[::-1]
     }
-    return [found[mask] for mask in masks]
+    return [found[mask] for mask in masks[::-1]]
 
 
 def tree_sum(parts):

time: 26.5 us -> 26.8 us (1.011); the launches traced: 26.8 us -> 26.6 us
  Pallas kernels: 9.39 us -> 6.7 us
  starting transfers between devices: 10.4 us -> 12.1 us
  waiting for transfers between devices: 5.55 us -> 6.41 us
    pallas_call x1, Pallas kernels: 2.18 us -> 1.12 us  [local(): call(forward_kernel, (shape((slots, probes, width), bf16), shape((probes...]
    pallas_call x1, Pallas kernels: 3.11 us -> 2.16 us  [local(): call(inner_kernel, (shape((2 * cols,) + column, f32), shape((2, rim) + co...]
    ppermute x2, starting transfers between devices: 7.63 us -> 8.57 us  [swapped_across(): lax.ppermute(half, 'orbit', [(i, (i + 2 * (i % 2) - 1) % count) for i in...]
    ppermute x5, waiting for transfers between devices: 5.54 us -> 6.4 us  [partners(): lax.ppermute(array, 'orbit', [(i, i ^ mask) for i in devices])]
    ppermute x5, starting transfers between devices: 2.77 us -> 3.49 us  [partners(): lax.ppermute(array, 'orbit', [(i, i ^ mask) for i in devices])]
    pallas_call x1, Pallas kernels: 1.79 us -> 1.11 us  [local(): call(backward_kernel, (whole, near, near), [SMEM()] * 3 + [VMEM()] * 6, d...]
  transfers between devices with their start and end apart: 9 -> 9, of which waited for: 3 -> 4; matrix products, arithmetic and copies ran while one was open for 0% -> 0% of each run, Pallas kernels for 18% -> 12%
where the time goes in v1:
time: 26.8 us; the launch traced here: 26.6 us
  starting transfers between devices  12.1 us (45%)
  Pallas kernels  6.7 us (25%)
  waiting for transfers between devices  6.41 us (24%)
  between operations  1.39 us (5%)
    ppermute x2, starting transfers between devices, swapped_across(): lax.ppermute(half, 'orbit', [(i, (i + 2 * (i % 2) - 1) % count) for i in...  8.57 us
    ppermute x5, waiting for transfers between devices, partners(): lax.ppermute(array, 'orbit', [(i, i ^ mask) for i in devices])  6.4 us
    ppermute x5, starting transfers between devices, partners(): lax.ppermute(array, 'orbit', [(i, i ^ mask) for i in devices])  3.49 us
    pallas_call x1, Pallas kernels, local(): call(inner_kernel, (shape((2 * cols,) + column, f32), shape((2, rim) + co...  2.16 us
    pallas_call x1, Pallas kernels, local(): call(final_kernel, (whole, whole, shape((1, probes), f32)), [VMEM()] * (6...  1.24 us
    pallas_call x1, Pallas kernels, local(): call(forward_kernel, (shape((slots, probes, width), bf16), shape((probes...  1.12 us
    pallas_call x1, Pallas kernels, local(): call(backward_kernel, (whole, near, near), [SMEM()] * 3 + [VMEM()] * 6, d...  1.11 us
    pallas_call x1, Pallas kernels, local(): call(rounding_kernel, (whole, near, near), [HBM()], 2 * elements, 10 * el...  1.07 us
  transfers between devices with their start and end apart: 9, of which 4 were waited for; matrix products, arithmetic and copies ran while one was open for 0% of the time, Pallas kernels for 12%

profile of v1, /device:TPU:0, one launch (start us, length us, event | category | flops | bytes accessed | tf_op | source)
XLA Modules:
  0.0 26.6 jit_solution(1782548297525428193)
XLA Ops:
  0.6 1.1 %shard_map.112 = (f32[8,8,16,128]{3,2,1,0:T(8,128)S(1)}, bf16[4,8,16,128]{3,2,1,0:T(8,128)(2,1)S(1)}, bf16[4,8,16,128]{3,2,1,0:T(8,128)(2,1)S(1)}) custom-call(f32[8,8,16,128]{3,2,1,0:T(8,128)} %direction.1), custom_call_target="tpu_custom_call" | custom-call | flops 262144 | bytes 1310720 | tf_op jit(solution)/shard_map/pallas_call | solution.py:304
  1.7 5.5 %collective-permute-start = (bf16[4,8,16,128]{3,2,1,0:T(8,128)(2,1)S(1)}, bf16[4,8,16,128]{3,2,1,0:T(8,128)(2,1)S(1)}, u32[]{:S(2)}, u32[]{:S(2)}) collective-permute-start(bf16[4,8,16,128]{3,2,1,0:T(8,128)(2,1)S(1)} %get-tuple-element.34.across), channel_id=1, source_target_pairs={{0,15},{1,2},{2,1},{3,4},{4,3},{5,6},{6,5},{7,8},{8,7},{9,10},{10,... | collective-permute-start | bytes 393224 | tf_op jit(solution)/shard_map/ppermute | solution.py:260
  7.2 0.0 collective-permute-start.1
  7.9 0.0 copy-start.3
  7.9 2.2 %shard_map.113 = (f32[16,8,16,128]{3,2,1,0:T(8,128)S(1)}, f32[2,4,8,16,128]{4,3,2,1,0:T(8,128)S(1)}, f32[16,128]{1,0:T(8,128)S(1)}, f32[16,128]{1,0:T(8,128)S(1)...) custom-call(f32[8,8,16,128]{3,2,1,0:T(8,128)S(1)} %get-tuple-element, ...), custom_call_target="tpu_custom_call" | custom-call | flops 7864320 | bytes 12582912 | tf_op jit(solution)/shard_map/pallas_call | solution.py:314
  10.1 0.0 collective-permute-done.from_across
  10.1 0.0 collective-permute-done.1.from_within
  10.1 0.0 copy-start
  10.1 0.0 copy-start.1
  10.1 0.0 copy-start.2
  10.1 1.1 %shard_map.114 = (bf16[8,16,128]{2,1,0:T(8,128)(2,1)S(1)}, f32[8,128]{1,0:T(8,128)S(1)}) custom-call(s32[8,24]{1,0:T(8,128)S(4)} %get-tuple-element.30.crossing, s32[8]{0:T(128)S(4)} %get-tuple-element.32.live, f32[8,128]{1,0:T(8,128)S(1)} %get-tuple-element.33.rows, bf16[4,8,16,128]{3,2,1,0:T(8,128)(2,1)S(1)} %get-tuple-element.34.across, ...), custom_call_target="tpu_custom_call" | custom-call | flops 100663296 | bytes 6291456 | tf_op jit(solution)/shard_map/pallas_call | solution.py:341
  11.2 0.5 %collective-permute-start.3 = (f32[8,128]{1,0:T(8,128)S(1)}, f32[8,128]{1,0:T(8,128)S(1)}, u32[]{:S(2)}, u32[]{:S(2)}) collective-permute-start(f32[8,128]{1,0:T(8,128)S(1)} %get-tuple-element.47), channel_id=1, source_target_pairs={{0,2},{1,3},{2,0},{3,1},{4,6},{5,7},{6,4},{7,5},{8,10},{9,11},{10,... | collective-permute-start | bytes 12296 | tf_op jit(solution)/shard_map/ppermute | solution.py:276
  11.7 0.0 copy-done.3
  11.7 1.1 %shard_map.115 = (f32[8,8,16,128]{3,2,1,0:T(8,128)S(1)}, bf16[4,8,16,128]{3,2,1,0:T(8,128)(2,1)S(1)}, bf16[4,8,16,128]{3,2,1,0:T(8,128)(2,1)S(1)}) custom-call(s32[8,24]{1,0:T(8,128)S(4)} %get-tuple-element.30.crossing, s32[128]{0:T(128)S(4)} %get-tuple-element.31.classes, s32[8]{0:T(128)S(4)} %get-tuple-element.32.live, f32[8,128]{1,0:T(8,128)S(1)} %copy-done.3, ...), custom_call_target="tpu_custom_call" | custom-call | flops 100663296 | bytes 6291456 | tf_op jit(solution)/shard_map/pallas_call | solution.py:352
  12.8 2.0 %collective-permute-done.3 = f32[8,128]{1,0:T(8,128)S(1)} collective-permute-done((f32[8,128]{1,0:T(8,128)S(1)}, f32[8,128]{1,0:T(8,128)S(1)}, u32[]{:S(2)}, u32[]{:S(2)}) %collective-permute-start.3) | collective-permute-done | bytes 4128 | tf_op jit(solution)/shard_map/ppermute | solution.py:276
  14.9 0.0 collective-permute-start.4
  14.9 3.1 %collective-permute-start.2 = (bf16[4,8,16,128]{3,2,1,0:T(8,128)(2,1)S(1)}, bf16[4,8,16,128]{3,2,1,0:T(8,128)(2,1)S(1)}, u32[]{:S(2)}, u32[]{:S(2)}) collective-permute-start(bf16[4,8,16,128]{3,2,1,0:T(8,128)(2,1)S(1)} %get-tuple-element.43), channel_id=1, source_target_pairs={{0,15},{1,2},{2,1},{3,4},{4,3},{5,6},{6,5},{7,8},{8,7},{9,10},{10,... | collective-permute-start | bytes 393224 | tf_op jit(solution)/shard_map/ppermute | solution.py:260
  17.9 0.5 %collective-permute-done.4 = f32[8,128]{1,0:T(8,128)S(1)} collective-permute-done((f32[8,128]{1,0:T(8,128)S(1)}, f32[8,128]{1,0:T(8,128)S(1)}, u32[]{:S(2)}, u32[]{:S(2)}) %collective-permute-start.4) | collective-permute-done | bytes 4128 | tf_op jit(solution)/shard_map/ppermute | solution.py:276
  18.5 0.0 collective-permute-start.5
  18.5 2.3 %collective-permute-start.6 = (f32[8,128]{1,0:T(8,128)S(1)}, f32[8,128]{1,0:T(8,128)S(1)}, u32[]{:S(2)}, u32[]{:S(2)}) collective-permute-start(f32[8,128]{1,0:T(8,128)S(1)} %add.7.rest_0_), channel_id=1, source_target_pairs={{0,9},{1,8},{2,11},{3,10},{4,13},{5,12},{6,15},{7,14},{8,1},{9,0},... | collective-permute-start | bytes 12296 | tf_op jit(solution)/shard_map/ppermute | solution.py:276
  20.8 0.7 %collective-permute-start.7 = (f32[8,128]{1,0:T(8,128)S(1)}, f32[8,128]{1,0:T(8,128)S(1)}, u32[]{:S(2)}, u32[]{:S(2)}) collective-permute-start(f32[8,128]{1,0:T(8,128)S(1)} %add.7.rest_0_), channel_id=1, source_target_pairs={{0,8},{1,9},{2,10},{3,11},{4,12},{5,13},{6,14},{7,15},{8,0},{9,1},... | collective-permute-start | bytes 12296 | tf_op jit(solution)/shard_map/ppermute | solution.py:276
  21.5 0.0 collective-permute-start.8
  21.5 0.9 %collective-permute-done.6.rest_1_ = f32[8,128]{1,0:T(8,128)S(1)} collective-permute-done((f32[8,128]{1,0:T(8,128)S(1)}, f32[8,128]{1,0:T(8,128)S(1)}, u32[]{:S(2)}, u32[]{:S(2)}) %collective-permute-start.6) | collective-permute-done | bytes 4128 | tf_op jit(solution)/shard_map/ppermute | solution.py:276
  22.4 2.9 %collective-permute-done.7.rest_2_ = f32[8,128]{1,0:T(8,128)S(1)} collective-permute-done((f32[8,128]{1,0:T(8,128)S(1)}, f32[8,128]{1,0:T(8,128)S(1)}, u32[]{:S(2)}, u32[]{:S(2)}) %collective-permute-start.7) | collective-permute-done | bytes 4128 | tf_op jit(solution)/shard_map/ppermute | solution.py:276
  25.3 0.0 collective-permute-done.8.rest_3_
  25.3 0.0 collective-permute-done.2.from_across
  25.3 0.0 collective-permute-done.5.from_within
  25.3 0.0 copy-done
  25.3 0.0 copy-done.1
  25.4 0.0 copy-done.2
  25.4 1.2 %shard_map.116 = (f32[8,8,16,128]{3,2,1,0:T(8,128)}, f32[8,8,16,128]{3,2,1,0:T(8,128)}, f32[1,16]{1,0:T(1,128)}) custom-call(f32[8,8,16,128]{3,2,1,0:T(8,128)S(1)} %copy-done.2, f32[8,8,16,128]{3,2,1,0:T(8,128)S(1)} %copy-done.1, f32[8,8,16,128]{3,2,1,0:T(8,128)S(1)} %copy-done, f32[8,8,16,128]{3,2,1,0:T(8,128)S(1)} %get-tuple-element.42.image, ...), custom_call_target="tpu_custom_call" | custom-call | flops 1048576 | bytes 3670016 | tf_op jit(solution)/shard_map/pallas_call | solution.py:373
  (2 shorter events, 0.0 us)
Async XLA Ops:
  1.7 8.4 %collective-permute-start = (bf16[4,8,16,128]{3,2,1,0:T(8,128)(2,1)S(1)}, bf16[4,8,16,128]{3,2,1,0:T(8,128)(2,1)S(1)}, u32[]{:S(2)}, u32[]{:S(2)}) collective-permute-start(bf16[4,8,16,128]{3,2,1,0:T(8,128)(2,1)S(1)} %get-tuple-element.34.across), channel_id=1, source_target_pairs={{0,15},{1,2},{2,1},{3,4},{4,3},{5,6},{6,5},{7,8},{8,7},{9,10},{10,... | collective-permute-start | bytes 393224 | tf_op jit(solution)/shard_map/ppermute | solution.py:260
  7.2 2.9 %collective-permute-start.1 = (bf16[4,8,16,128]{3,2,1,0:T(8,128)(2,1)S(1)}, bf16[4,8,16,128]{3,2,1,0:T(8,128)(2,1)S(1)}, u32[]{:S(2)}, u32[]{:S(2)}) collective-permute-start(bf16[4,8,16,128]{3,2,1,0:T(8,128)(2,1)S(1)} %get-tuple-element.35.within), channel_id=1, source_target_pairs={{0,1},{1,0},{2,3},{3,2},{4,5},{5,4},{6,7},{7,6},{8,9},{9,8},{10,11... | collective-permute-start | bytes 393224 | tf_op jit(solution)/shard_map/ppermute | solution.py:264
  7.9 3.8 %copy-start.3 = (f32[8,128]{1,0:T(8,128)S(1)}, f32[8,128]{1,0:T(8,128)}, u32[]{:S(2)}) copy-start(f32[8,128]{1,0:T(8,128)} %smooth.1) | copy-start | bytes 12292
  10.1 15.3 %copy-start = (f32[8,8,16,128]{3,2,1,0:T(8,128)S(1)}, f32[8,8,16,128]{3,2,1,0:T(8,128)}, u32[]{:S(2)}) copy-start(f32[8,8,16,128]{3,2,1,0:T(8,128)} %direction.1) | copy-start | bytes 1572868
  10.1 15.3 %copy-start.1 = (f32[8,8,16,128]{3,2,1,0:T(8,128)S(1)}, f32[8,8,16,128]{3,2,1,0:T(8,128)}, u32[]{:S(2)}) copy-start(f32[8,8,16,128]{3,2,1,0:T(8,128)} %residual.1) | copy-start | bytes 1572868
  10.1 15.3 %copy-start.2 = (f32[8,8,16,128]{3,2,1,0:T(8,128)S(1)}, f32[8,8,16,128]{3,2,1,0:T(8,128)}, u32[]{:S(2)}) copy-start(f32[8,8,16,128]{3,2,1,0:T(8,128)} %solution.1) | copy-start | bytes 1572868
  11.2 3.6 %collective-permute-start.3 = (f32[8,128]{1,0:T(8,128)S(1)}, f32[8,128]{1,0:T(8,128)S(1)}, u32[]{:S(2)}, u32[]{:S(2)}) collective-permute-start(f32[8,128]{1,0:T(8,128)S(1)} %get-tuple-element.47), channel_id=1, source_target_pairs={{0,2},{1,3},{2,0},{3,1},{4,6},{5,7},{6,4},{7,5},{8,10},{9,11},{10,... | collective-permute-start | bytes 12296 | tf_op jit(solution)/shard_map/ppermute | solution.py:276
  14.9 3.6 %collective-permute-start.4 = (f32[8,128]{1,0:T(8,128)S(1)}, f32[8,128]{1,0:T(8,128)S(1)}, u32[]{:S(2)}, u32[]{:S(2)}) collective-permute-start(f32[8,128]{1,0:T(8,128)S(1)} %add.6), channel_id=1, source_target_pairs={{0,4},{1,5},{2,6},{3,7},{4,0},{5,1},{6,2},{7,3},{8,12},{9,13},{10,... | collective-permute-start | bytes 12296 | tf_op jit(solution)/shard_map/ppermute | solution.py:276
  14.9 10.5 %collective-permute-start.2 = (bf16[4,8,16,128]{3,2,1,0:T(8,128)(2,1)S(1)}, bf16[4,8,16,128]{3,2,1,0:T(8,128)(2,1)S(1)}, u32[]{:S(2)}, u32[]{:S(2)}) collective-permute-start(bf16[4,8,16,128]{3,2,1,0:T(8,128)(2,1)S(1)} %get-tuple-element.43), channel_id=1, source_target_pairs={{0,15},{1,2},{2,1},{3,4},{4,3},{5,6},{6,5},{7,8},{8,7},{9,10},{10,... | collective-permute-start | bytes 393224 | tf_op jit(solution)/shard_map/ppermute | solution.py:260
  18.5 6.9 %collective-permute-start.5 = (bf16[4,8,16,128]{3,2,1,0:T(8,128)(2,1)S(1)}, bf16[4,8,16,128]{3,2,1,0:T(8,128)(2,1)S(1)}, u32[]{:S(2)}, u32[]{:S(2)}) collective-permute-start(bf16[4,8,16,128]{3,2,1,0:T(8,128)(2,1)S(1)} %get-tuple-element.49), channel_id=1, source_target_pairs={{0,1},{1,0},{2,3},{3,2},{4,5},{5,4},{6,7},{7,6},{8,9},{9,8},{10,11... | collective-permute-start | bytes 393224 | tf_op jit(solution)/shard_map/ppermute | solution.py:264
  18.5 3.9 %collective-permute-start.6 = (f32[8,128]{1,0:T(8,128)S(1)}, f32[8,128]{1,0:T(8,128)S(1)}, u32[]{:S(2)}, u32[]{:S(2)}) collective-permute-start(f32[8,128]{1,0:T(8,128)S(1)} %add.7.rest_0_), channel_id=1, source_target_pairs={{0,9},{1,8},{2,11},{3,10},{4,13},{5,12},{6,15},{7,14},{8,1},{9,0},... | collective-permute-start | bytes 12296 | tf_op jit(solution)/shard_map/ppermute | solution.py:276
  20.8 4.5 %collective-permute-start.7 = (f32[8,128]{1,0:T(8,128)S(1)}, f32[8,128]{1,0:T(8,128)S(1)}, u32[]{:S(2)}, u32[]{:S(2)}) collective-permute-start(f32[8,128]{1,0:T(8,128)S(1)} %add.7.rest_0_), channel_id=1, source_target_pairs={{0,8},{1,9},{2,10},{3,11},{4,12},{5,13},{6,14},{7,15},{8,0},{9,1},... | collective-permute-start | bytes 12296 | tf_op jit(solution)/shard_map/ppermute | solution.py:276
  21.5 3.8 %collective-permute-start.8 = (f32[8,128]{1,0:T(8,128)S(1)}, f32[8,128]{1,0:T(8,128)S(1)}, u32[]{:S(2)}, u32[]{:S(2)}) collective-permute-start(f32[8,128]{1,0:T(8,128)S(1)} %add.7.rest_0_), channel_id=1, source_target_pairs={{0,1},{1,0},{2,3},{3,2},{4,5},{5,4},{6,7},{7,6},{8,9},{9,8},{10,11... | collective-permute-start | bytes 12296 | tf_op jit(solution)/shard_map/ppermute | solution.py:276

commit v2 on v1

--- a/solution.py
+++ b/solution.py
@@ -47,21 +47,13 @@
     return lax.rem(lax.axis_index("orbit"), 2)
 
 
-def rounding_kernel(direction_hbm, direction, across, within, sems):
-    rim = across.shape[0]
-    odd = parity()
-    halves = ((odd, across), (1 - odd, within))
-    copies = []
-    for k, (place, _) in enumerate(halves):
-        half = pl.ds(place * rim, rim)
-        copies.append(
-            pltpu.make_async_copy(direction_hbm.at[half], direction.at[half], sems.at[k])
-        )
-        copies[-1].start()
-    for copy, (place, half) in zip(copies, halves):
-        copy.wait()
-        for c in range(rim):
-            half[c] = masked(direction[place * rim + c]).astype(jnp.bfloat16)
+def rounding_kernel(leaves, direction_hbm, direction, half, sem):
+    rim = half.shape[0]
+    place = pl.ds((parity() if leaves else 1 - parity()) * rim, rim)
+    copy = pltpu.make_async_copy(direction_hbm.at[place], direction, sem)
+    copy.start()
+    copy.wait()
+    half[...] = masked(direction[...]).astype(jnp.bfloat16)
 
 
 def coupling(classes, cols, columns):
@@ -96,8 +88,9 @@
 
 
 def inner_kernel(
-    direction, count, residual_hbm, classes_hbm, smooth_hbm, sight_hbm, crossing_hbm, jac_hbm,
-    begun, faced, norm, curved, rows, jac, crossing, classes, live, residual, smooth, sight, sems,
+    leaving, staying, count, residual_hbm, classes_hbm, smooth_hbm, sight_hbm, crossing_hbm, jac_hbm,
+    begun, faced, norm, curved, rows, jac, crossing, classes, live,
+    direction, residual, smooth, sight, sems,
 ):
     pairs = (
         (classes_hbm, classes), (smooth_hbm, smooth), (sight_hbm, sight),
@@ -118,8 +111,11 @@
     live[0] = count[0]
     copies[0].wait()
     copies[1].wait()
-    cols = direction.shape[0]
-    rim = cols // 2
+    rim = leaving.shape[0]
+    cols = 2 * rim
+    odd = parity()
+    direction[pl.ds(odd * rim, rim)] = leaving[...]
+    direction[pl.ds((1 - odd) * rim, rim)] = staying[...]
     table = coupling(classes, cols, range(-REACH, cols))
     weight = smooth[...][:, None, :]
     total = jnp.zeros(norm.shape, jnp.float32)
@@ -301,14 +297,18 @@
     whole = shape(direction.shape, f32)
     small = shape((probes, width), f32)
 
-    held, across, within = call(
-        rounding_kernel,
-        (whole, near, near),
-        [HBM()],
-        2 * elements,
-        10 * elements,
-        [pltpu.SemaphoreType.DMA((2,))],
-    )(in_hbm(direction))
+    halves = [
+        call(
+            functools.partial(rounding_kernel, leaves),
+            (shape(near.shape, f32), near),
+            [HBM()],
+            elements,
+            5 * elements,
+            [pltpu.SemaphoreType.DMA],
+        )(in_hbm(direction))
+        for leaves in (True, False)
+    ]
+    (leaving, across), (staying, within) = halves
     from_across, from_within = swapped_across(across), swapped_within(within)
 
     begun, faced, norm, curved, rows, jac, crossing, length_class, live = call(
@@ -319,10 +319,11 @@
             pltpu.SMEM(crossing.shape, jnp.int32), pltpu.SMEM(length_class.shape, jnp.int32),
             pltpu.SMEM((8,), jnp.int32),
         ),
-        [VMEM(), SMEM()] + [HBM()] * 6,
+        [VMEM(), VMEM(), SMEM()] + [HBM()] * 6,
         60 * elements,
         4 * jacobian.size,
         [
+            pltpu.VMEM(direction.shape, f32),
             pltpu.VMEM(direction.shape, f32),
             pltpu.VMEM(smooth_weight.shape, f32),
             pltpu.VMEM(sightline_weight.shape, f32),
@@ -330,7 +331,7 @@
         ],
         [VMEM()] * 6 + [SMEM()] * 3,
     )(
-        held, tile_count,
+        leaving, staying, tile_count,
         *map(in_hbm, (
             residual, length_class, smooth_weight, sightline_weight, crossing, jacobian,
         )),
@@ -364,7 +365,6 @@
     within, *held = lax.optimization_barrier((within, *held))
     sums = tree_sum(held)
     held = [sums] + partners(sums, far_steps[0])
-    within, *held = lax.optimization_barrier((within, *held))
     from_within = swapped_within(within)
     for step in far_steps[1:]:
         sums = tree_sum(held)

time: 26.8 us -> 27 us (level)
  waiting for transfers between devices: 6.41 us -> 5.39 us
  Pallas kernels: 6.7 us -> 7.59 us
  starting transfers between devices: 12.1 us -> 12.5 us
    ppermute x2, starting transfers between devices: 8.57 us -> 9.6 us  [swapped_across(): lax.ppermute(half, 'orbit', [(i, (i + 2 * (i % 2) - 1) % count) for i in...]
    ppermute x5, waiting for transfers between devices: 6.4 us -> 5.38 us  [partners(): lax.ppermute(array, 'orbit', [(i, i ^ mask) for i in devices])]
    pallas_call x1 -> x2, Pallas kernels: 1.07 us -> 1.96 us  [local(): call(functools.partial(rounding_kernel, leaves), (shape(near.shape, f32),...]
    ppermute x5, starting transfers between devices: 3.49 us -> 2.84 us  [partners(): lax.ppermute(array, 'orbit', [(i, i ^ mask) for i in devices])]
  transfers between devices with their start and end apart: 9 -> 9, of which waited for: 4 -> 3; matrix products, arithmetic and copies ran while one was open for 0% -> 0% of each run, Pallas kernels for 12% -> 16%
where the time goes in v2:
time: 27 us
  starting transfers between devices  12.5 us (46%)
  Pallas kernels  7.59 us (28%)
  waiting for transfers between devices  5.39 us (20%)
  between operations  1.42 us (5%)
    ppermute x2, starting transfers between devices, swapped_across(): lax.ppermute(half, 'orbit', [(i, (i + 2 * (i % 2) - 1) % count) for i in...  9.6 us
    ppermute x5, waiting for transfers between devices, partners(): lax.ppermute(array, 'orbit', [(i, i ^ mask) for i in devices])  5.38 us
    ppermute x5, starting transfers between devices, partners(): lax.ppermute(array, 'orbit', [(i, i ^ mask) for i in devices])  2.84 us
    pallas_call x1, Pallas kernels, local(): call(inner_kernel, (shape((2 * cols,) + column, f32), shape((2, rim) + co...  2.17 us
    pallas_call x2, Pallas kernels, local(): call(functools.partial(rounding_kernel, leaves), (shape(near.shape, f32),...  1.96 us
    pallas_call x1, Pallas kernels, local(): call(final_kernel, (whole, whole, shape((1, probes), f32)), [VMEM()] * (6...  1.24 us
    pallas_call x1, Pallas kernels, local(): call(forward_kernel, (shape((slots, probes, width), bf16), shape((probes...  1.12 us
    pallas_call x1, Pallas kernels, local(): call(backward_kernel, (whole, near, near), [SMEM()] * 3 + [VMEM()] * 6, d...  1.11 us
  transfers between devices with their start and end apart: 9, of which 3 were waited for; matrix products, arithmetic and copies ran while one was open for 0% of the time, Pallas kernels for 16%

profile of v2, /device:TPU:0, one launch (start us, length us, event | category | flops | bytes accessed | tf_op | source)
XLA Modules:
  0.0 27.0 jit_solution(5224775673041441458)
XLA Ops:
  0.6 1.0 %shard_map.112 = (f32[4,8,16,128]{3,2,1,0:T(8,128)S(1)}, bf16[4,8,16,128]{3,2,1,0:T(8,128)(2,1)S(1)}) custom-call(f32[8,8,16,128]{3,2,1,0:T(8,128)} %direction.1), custom_call_target="tpu_custom_call" | custom-call | flops 131072 | bytes 655360 | tf_op jit(solution)/shard_map/pallas_call | solution.py:301
  1.6 5.5 %collective-permute-start = (bf16[4,8,16,128]{3,2,1,0:T(8,128)(2,1)S(1)}, bf16[4,8,16,128]{3,2,1,0:T(8,128)(2,1)S(1)}, u32[]{:S(2)}, u32[]{:S(2)}) collective-permute-start(bf16[4,8,16,128]{3,2,1,0:T(8,128)(2,1)S(1)} %get-tuple-element.33.across), channel_id=1, source_target_pairs={{0,15},{1,2},{2,1},{3,4},{4,3},{5,6},{6,5},{7,8},{8,7},{9,10},{10,... | collective-permute-start | bytes 393224 | tf_op jit(solution)/shard_map/ppermute | solution.py:256
  7.1 1.0 %shard_map.113 = (f32[4,8,16,128]{3,2,1,0:T(8,128)S(1)}, bf16[4,8,16,128]{3,2,1,0:T(8,128)(2,1)S(1)}) custom-call(f32[8,8,16,128]{3,2,1,0:T(8,128)} %direction.1), custom_call_target="tpu_custom_call" | custom-call | flops 131072 | bytes 655360 | tf_op jit(solution)/shard_map/pallas_call | solution.py:301
  8.1 0.1 collective-permute-start.1
  8.8 0.0 copy-start.3
  8.9 2.2 %shard_map.114 = (f32[16,8,16,128]{3,2,1,0:T(8,128)S(1)}, f32[2,4,8,16,128]{4,3,2,1,0:T(8,128)S(1)}, f32[16,128]{1,0:T(8,128)S(1)}, f32[16,128]{1,0:T(8,128)S(1)...) custom-call(f32[4,8,16,128]{3,2,1,0:T(8,128)S(1)} %get-tuple-element, ...), custom_call_target="tpu_custom_call" | custom-call | flops 7864320 | bytes 12582912 | tf_op jit(solution)/shard_map/pallas_call | solution.py:314
  11.0 0.0 collective-permute-done.from_across
  11.0 0.0 collective-permute-done.1.from_within
  11.0 0.0 copy-start
  11.1 0.0 copy-start.1
  11.1 0.0 copy-start.2
  11.1 1.1 %shard_map.115 = (bf16[8,16,128]{2,1,0:T(8,128)(2,1)S(1)}, f32[8,128]{1,0:T(8,128)S(1)}) custom-call(s32[8,24]{1,0:T(8,128)S(4)} %get-tuple-element.29.crossing, s32[8]{0:T(128)S(4)} %get-tuple-element.31.live, f32[8,128]{1,0:T(8,128)S(1)} %get-tuple-element.32.rows, bf16[4,8,16,128]{3,2,1,0:T(8,128)(2,1)S(1)} %get-tuple-element.33.across, ...), custom_call_target="tpu_custom_call" | custom-call | flops 100663296 | bytes 6291456 | tf_op jit(solution)/shard_map/pallas_call | solution.py:342
  12.2 0.0 collective-permute-start.3
  12.2 0.0 copy-done.3
  12.2 1.1 %shard_map.116 = (f32[8,8,16,128]{3,2,1,0:T(8,128)S(1)}, bf16[4,8,16,128]{3,2,1,0:T(8,128)(2,1)S(1)}, bf16[4,8,16,128]{3,2,1,0:T(8,128)(2,1)S(1)}) custom-call(s32[8,24]{1,0:T(8,128)S(4)} %get-tuple-element.29.crossing, s32[128]{0:T(128)S(4)} %get-tuple-element.30.classes, s32[8]{0:T(128)S(4)} %get-tuple-element.31.live, f32[8,128]{1,0:T(8,128)S(1)} %copy-done.3, ...), custom_call_target="tpu_custom_call" | custom-call | flops 100663296 | bytes 6291456 | tf_op jit(solution)/shard_map/pallas_call | solution.py:353
  13.3 4.1 %collective-permute-start.2 = (bf16[4,8,16,128]{3,2,1,0:T(8,128)(2,1)S(1)}, bf16[4,8,16,128]{3,2,1,0:T(8,128)(2,1)S(1)}, u32[]{:S(2)}, u32[]{:S(2)}) collective-permute-start(bf16[4,8,16,128]{3,2,1,0:T(8,128)(2,1)S(1)} %get-tuple-element.42), channel_id=1, source_target_pairs={{0,15},{1,2},{2,1},{3,4},{4,3},{5,6},{6,5},{7,8},{8,7},{9,10},{10,... | collective-permute-start | bytes 393224 | tf_op jit(solution)/shard_map/ppermute | solution.py:256
  17.4 0.0 collective-permute-done.3
  17.4 0.0 collective-permute-start.4
  17.5 0.1 collective-permute-start.5
  17.5 3.6 %collective-permute-done.5 = f32[8,128]{1,0:T(8,128)S(1)} collective-permute-done((f32[8,128]{1,0:T(8,128)S(1)}, f32[8,128]{1,0:T(8,128)S(1)}, u32[]{:S(2)}, u32[]{:S(2)}) %collective-permute-start.5) | collective-permute-done | bytes 4128 | tf_op jit(solution)/shard_map/ppermute | solution.py:272
  21.1 0.0 collective-permute-start.6
  21.1 2.0 %collective-permute-start.7 = (f32[8,128]{1,0:T(8,128)S(1)}, f32[8,128]{1,0:T(8,128)S(1)}, u32[]{:S(2)}, u32[]{:S(2)}) collective-permute-start(f32[8,128]{1,0:T(8,128)S(1)} %add.7.rest_0_), channel_id=1, source_target_pairs={{0,8},{1,9},{2,10},{3,11},{4,12},{5,13},{6,14},{7,15},{8,0},{9,1},... | collective-permute-start | bytes 12296 | tf_op jit(solution)/shard_map/ppermute | solution.py:272
  23.2 0.7 %collective-permute-start.8 = (f32[8,128]{1,0:T(8,128)S(1)}, f32[8,128]{1,0:T(8,128)S(1)}, u32[]{:S(2)}, u32[]{:S(2)}) collective-permute-start(f32[8,128]{1,0:T(8,128)S(1)} %add.7.rest_0_), channel_id=1, source_target_pairs={{0,1},{1,0},{2,3},{3,2},{4,5},{5,4},{6,7},{7,6},{8,9},{9,8},{10,11... | collective-permute-start | bytes 12296 | tf_op jit(solution)/shard_map/ppermute | solution.py:272
  23.9 1.2 %collective-permute-done.6.rest_1_ = f32[8,128]{1,0:T(8,128)S(1)} collective-permute-done((f32[8,128]{1,0:T(8,128)S(1)}, f32[8,128]{1,0:T(8,128)S(1)}, u32[]{:S(2)}, u32[]{:S(2)}) %collective-permute-start.6) | collective-permute-done | bytes 4128 | tf_op jit(solution)/shard_map/ppermute | solution.py:272
  25.1 0.6 %collective-permute-done.7.rest_2_ = f32[8,128]{1,0:T(8,128)S(1)} collective-permute-done((f32[8,128]{1,0:T(8,128)S(1)}, f32[8,128]{1,0:T(8,128)S(1)}, u32[]{:S(2)}, u32[]{:S(2)}) %collective-permute-start.7) | collective-permute-done | bytes 4128 | tf_op jit(solution)/shard_map/ppermute | solution.py:272
  25.7 0.0 collective-permute-done.8.rest_3_
  25.7 0.0 collective-permute-done.2.from_across
  25.7 0.0 collective-permute-done.4.from_within
  25.7 0.0 copy-done
  25.7 0.0 copy-done.1
  25.7 0.0 copy-done.2
  25.7 1.2 %shard_map.117 = (f32[8,8,16,128]{3,2,1,0:T(8,128)}, f32[8,8,16,128]{3,2,1,0:T(8,128)}, f32[1,16]{1,0:T(1,128)}) custom-call(f32[8,8,16,128]{3,2,1,0:T(8,128)S(1)} %copy-done.2, f32[8,8,16,128]{3,2,1,0:T(8,128)S(1)} %copy-done.1, f32[8,8,16,128]{3,2,1,0:T(8,128)S(1)} %copy-done, f32[8,8,16,128]{3,2,1,0:T(8,128)S(1)} %get-tuple-element.41.image, ...), custom_call_target="tpu_custom_call" | custom-call | flops 1048576 | bytes 3670016 | tf_op jit(solution)/shard_map/pallas_call | solution.py:373
  (2 shorter events, 0.0 us)
Async XLA Ops:
  1.6 9.4 %collective-permute-start = (bf16[4,8,16,128]{3,2,1,0:T(8,128)(2,1)S(1)}, bf16[4,8,16,128]{3,2,1,0:T(8,128)(2,1)S(1)}, u32[]{:S(2)}, u32[]{:S(2)}) collective-permute-start(bf16[4,8,16,128]{3,2,1,0:T(8,128)(2,1)S(1)} %get-tuple-element.33.across), channel_id=1, source_target_pairs={{0,15},{1,2},{2,1},{3,4},{4,3},{5,6},{6,5},{7,8},{8,7},{9,10},{10,... | collective-permute-start | bytes 393224 | tf_op jit(solution)/shard_map/ppermute | solution.py:256
  8.1 2.9 %collective-permute-start.1 = (bf16[4,8,16,128]{3,2,1,0:T(8,128)(2,1)S(1)}, bf16[4,8,16,128]{3,2,1,0:T(8,128)(2,1)S(1)}, u32[]{:S(2)}, u32[]{:S(2)}) collective-permute-start(bf16[4,8,16,128]{3,2,1,0:T(8,128)(2,1)S(1)} %get-tuple-element.34.within), channel_id=1, source_target_pairs={{0,1},{1,0},{2,3},{3,2},{4,5},{5,4},{6,7},{7,6},{8,9},{9,8},{10,11... | collective-permute-start | bytes 393224 | tf_op jit(solution)/shard_map/ppermute | solution.py:260
  8.8 3.4 %copy-start.3 = (f32[8,128]{1,0:T(8,128)S(1)}, f32[8,128]{1,0:T(8,128)}, u32[]{:S(2)}) copy-start(f32[8,128]{1,0:T(8,128)} %smooth.1) | copy-start | bytes 12292
  11.0 14.6 %copy-start = (f32[8,8,16,128]{3,2,1,0:T(8,128)S(1)}, f32[8,8,16,128]{3,2,1,0:T(8,128)}, u32[]{:S(2)}) copy-start(f32[8,8,16,128]{3,2,1,0:T(8,128)} %direction.1) | copy-start | bytes 1572868
  11.1 14.6 %copy-start.1 = (f32[8,8,16,128]{3,2,1,0:T(8,128)S(1)}, f32[8,8,16,128]{3,2,1,0:T(8,128)}, u32[]{:S(2)}) copy-start(f32[8,8,16,128]{3,2,1,0:T(8,128)} %residual.1) | copy-start | bytes 1572868
  11.1 14.6 %copy-start.2 = (f32[8,8,16,128]{3,2,1,0:T(8,128)S(1)}, f32[8,8,16,128]{3,2,1,0:T(8,128)}, u32[]{:S(2)}) copy-start(f32[8,8,16,128]{3,2,1,0:T(8,128)} %solution.1) | copy-start | bytes 1572868
  12.2 5.2 %collective-permute-start.3 = (f32[8,128]{1,0:T(8,128)S(1)}, f32[8,128]{1,0:T(8,128)S(1)}, u32[]{:S(2)}, u32[]{:S(2)}) collective-permute-start(f32[8,128]{1,0:T(8,128)S(1)} %get-tuple-element.46), channel_id=1, source_target_pairs={{0,2},{1,3},{2,0},{3,1},{4,6},{5,7},{6,4},{7,5},{8,10},{9,11},{10,... | collective-permute-start | bytes 12296 | tf_op jit(solution)/shard_map/ppermute | solution.py:272
  13.3 12.3 %collective-permute-start.2 = (bf16[4,8,16,128]{3,2,1,0:T(8,128)(2,1)S(1)}, bf16[4,8,16,128]{3,2,1,0:T(8,128)(2,1)S(1)}, u32[]{:S(2)}, u32[]{:S(2)}) collective-permute-start(bf16[4,8,16,128]{3,2,1,0:T(8,128)(2,1)S(1)} %get-tuple-element.42), channel_id=1, source_target_pairs={{0,15},{1,2},{2,1},{3,4},{4,3},{5,6},{6,5},{7,8},{8,7},{9,10},{10,... | collective-permute-start | bytes 393224 | tf_op jit(solution)/shard_map/ppermute | solution.py:256
  17.4 8.2 %collective-permute-start.4 = (bf16[4,8,16,128]{3,2,1,0:T(8,128)(2,1)S(1)}, bf16[4,8,16,128]{3,2,1,0:T(8,128)(2,1)S(1)}, u32[]{:S(2)}, u32[]{:S(2)}) collective-permute-start(bf16[4,8,16,128]{3,2,1,0:T(8,128)(2,1)S(1)} %get-tuple-element.45), channel_id=1, source_target_pairs={{0,1},{1,0},{2,3},{3,2},{4,5},{5,4},{6,7},{7,6},{8,9},{9,8},{10,11... | collective-permute-start | bytes 393224 | tf_op jit(solution)/shard_map/ppermute | solution.py:260
  17.5 3.7 %collective-permute-start.5 = (f32[8,128]{1,0:T(8,128)S(1)}, f32[8,128]{1,0:T(8,128)S(1)}, u32[]{:S(2)}, u32[]{:S(2)}) collective-permute-start(f32[8,128]{1,0:T(8,128)S(1)} %add.6), channel_id=1, source_target_pairs={{0,4},{1,5},{2,6},{3,7},{4,0},{5,1},{6,2},{7,3},{8,12},{9,13},{10,... | collective-permute-start | bytes 12296 | tf_op jit(solution)/shard_map/ppermute | solution.py:272
  21.1 3.9 %collective-permute-start.6 = (f32[8,128]{1,0:T(8,128)S(1)}, f32[8,128]{1,0:T(8,128)S(1)}, u32[]{:S(2)}, u32[]{:S(2)}) collective-permute-start(f32[8,128]{1,0:T(8,128)S(1)} %add.7.rest_0_), channel_id=1, source_target_pairs={{0,9},{1,8},{2,11},{3,10},{4,13},{5,12},{6,15},{7,14},{8,1},{9,0},... | collective-permute-start | bytes 12296 | tf_op jit(solution)/shard_map/ppermute | solution.py:272
  21.1 4.5 %collective-permute-start.7 = (f32[8,128]{1,0:T(8,128)S(1)}, f32[8,128]{1,0:T(8,128)S(1)}, u32[]{:S(2)}, u32[]{:S(2)}) collective-permute-start(f32[8,128]{1,0:T(8,128)S(1)} %add.7.rest_0_), channel_id=1, source_target_pairs={{0,8},{1,9},{2,10},{3,11},{4,12},{5,13},{6,14},{7,15},{8,0},{9,1},... | collective-permute-start | bytes 12296 | tf_op jit(solution)/shard_map/ppermute | solution.py:272
  23.2 2.5 %collective-permute-start.8 = (f32[8,128]{1,0:T(8,128)S(1)}, f32[8,128]{1,0:T(8,128)S(1)}, u32[]{:S(2)}, u32[]{:S(2)}) collective-permute-start(f32[8,128]{1,0:T(8,128)S(1)} %add.7.rest_0_), channel_id=1, source_target_pairs={{0,1},{1,0},{2,3},{3,2},{4,5},{5,4},{6,7},{7,6},{8,9},{9,8},{10,11... | collective-permute-start | bytes 12296 | tf_op jit(solution)/shard_map/ppermute | solution.py:272

commit v3 on v0

--- a/solution.py
+++ b/solution.py
@@ -88,6 +88,15 @@
     return [range(i, min(i + GROUP, slots)) for i in range(0, slots, GROUP)]
 
 
+def early_slots(slots):
+    return slot_groups(slots)[-1][0] if slots > GROUP else slots
+
+
+def slot_tiles(jac, late, i):
+    part, row = (jac, i) if i < jac.shape[0] else (late, i - jac.shape[0])
+    return jnp.concatenate([part[row, j] for j in range(part.shape[1])], axis=1)
+
+
 def if_live(count, group, work):
     if group[0] == 0:
         work()
@@ -113,7 +122,8 @@
             jac_hbm.at[part], jac.at[part], sems.at[len(pairs) + group[0] // GROUP]
         )
 
-    for group in slot_groups(jac.shape[0]):
+    early = slot_groups(jac.shape[0])
+    for group in early:
         if_live(count[0], group, lambda: load(group).start())
     live[0] = count[0]
     copies[0].wait()
@@ -154,15 +164,18 @@
         squares = squares + jnp.sum(mres * mres, axis=0)
     norm[...] = squares
     copies[4].wait()
-    for group in slot_groups(jac.shape[0]):
+    for group in early:
         if_live(count[0], group, lambda: load(group).wait())
 
 
 def forward_kernel(
-    crossing, live, rows, across, within, from_across, from_within, faced, norm, curved, jac,
-    weighted, sums, window, total,
+    crossing, live, rows, across, within, from_across, from_within, faced, norm, curved, jac, jac_hbm,
+    weighted, sums, late, window, total, sem,
 ):
     slots, crossings = crossing.shape
+    last = slot_groups(slots)[-1]
+    load = pltpu.make_async_copy(jac_hbm.at[pl.ds(last[0], len(last))], late, sem)
+    if_live(live[0], last, load.start)
     rim, species = across.shape[:2]
     span = rim * species
     odd = parity()
@@ -176,10 +189,12 @@
     total[...] = edges
 
     def project(group):
+        if group == last:
+            load.wait()
         added = jnp.zeros(total.shape, jnp.float32)
         for i in group:
             picked = jnp.concatenate([window[crossing[i, j]] for j in range(crossings)], axis=1)
-            tiles = jnp.concatenate([jac[i, j] for j in range(crossings)], axis=1)
+            tiles = slot_tiles(jac, late, i)
             integrals = lax.dot_general(
                 picked, tiles, (((1,), (1,)), ((), ())), preferred_element_type=jnp.float32
             )
@@ -201,7 +216,7 @@
 
 
 def backward_kernel(
-    crossing, classes, live, smooth, weighted, jac, begun, from_across, from_within,
+    crossing, classes, live, smooth, weighted, jac, late, begun, from_across, from_within,
     image, across, within, sums, near,
 ):
     slots, crossings = crossing.shape
@@ -222,7 +237,7 @@
 
     def project(group):
         for i in group:
-            tiles = jnp.concatenate([jac[i, j] for j in range(crossings)], axis=1)
+            tiles = slot_tiles(jac, late, i)
             terms = jnp.dot(weighted[i], tiles, preferred_element_type=jnp.float32)
             for j in range(crossings):
                 sums[crossing[i, j]] += terms[:, j * tile : (j + 1) * tile]
@@ -237,7 +252,7 @@
 def final_kernel(
     solution, residual, direction, image, from_across, from_within, *rest
 ):
-    *held, solution_next, residual_next, step_length = rest
+    *held, solution_out, residual_out, step_length, solution_next, residual_next, sems = rest
     whole = tree_sum([part[...] for part in held])
     norm = jnp.concatenate([whole[:, 0:1], whole[:, 2:3]], axis=0)
     curvature = jnp.concatenate([whole[:, 1:2], whole[:, 3:4]], axis=0)
@@ -247,11 +262,20 @@
     step_length[...] = jnp.transpose(wide)[0:1]
     wide = wide[None]
     odd = parity()
+    copies = [
+        pltpu.make_async_copy(solution_next, solution_out, sems.at[0]),
+        pltpu.make_async_copy(residual_next, residual_out, sems.at[1]),
+    ]
+    for c in range(2 * rim):
+        solution_next[c] = masked(solution[c] + wide * direction[c])
+    copies[0].start()
     for q in range(rim):
         for c, part in (odd * rim + q, from_across), ((1 - odd) * rim + q, from_within):
             total = masked(image[c] + part[q].astype(jnp.float32))
-            solution_next[c] = masked(solution[c] + wide * direction[c])
             residual_next[c] = masked(residual[c]) - wide * total
+    copies[1].start()
+    for copy in copies:
+        copy.wait()
 
 
 def swapped_across(half):
@@ -292,6 +316,7 @@
     assert REACH <= cols
     rim = cols // 2
     slots = crossing.shape[0]
+    early = early_slots(slots)
     f32, bf16 = jnp.float32, jnp.bfloat16
     shape = jax.ShapeDtypeStruct
     column = (species, probes, width)
@@ -315,7 +340,7 @@
         inner_kernel,
         (
             shape((2 * cols,) + column, f32), shape((2, rim) + column, f32), small, small,
-            shape(sightline_weight.shape, f32), shape(jacobian.shape, bf16),
+            shape(sightline_weight.shape, f32), shape((early,) + jacobian.shape[1:], bf16),
             pltpu.SMEM(crossing.shape, jnp.int32), pltpu.SMEM(length_class.shape, jnp.int32),
             pltpu.SMEM((8,), jnp.int32),
         ),
@@ -326,7 +351,7 @@
             pltpu.VMEM(direction.shape, f32),
             pltpu.VMEM(smooth_weight.shape, f32),
             pltpu.VMEM(sightline_weight.shape, f32),
-            pltpu.SemaphoreType.DMA((5 + len(slot_groups(slots)),)),
+            pltpu.SemaphoreType.DMA((5 + len(slot_groups(early)),)),
         ],
         [VMEM()] * 6 + [SMEM()] * 3,
     )(
@@ -338,28 +363,38 @@
 
     devices = lax.axis_size("orbit")
     peers = devices // 2
-    weighted, sums = call(
+    weighted, sums, late = call(
         forward_kernel,
-        (shape((slots, probes, width), bf16), shape((probes // 2, width), f32)),
-        [SMEM()] * 2 + [VMEM()] * 9,
+        (
+            shape((slots, probes, width), bf16), shape((probes // 2, width), f32),
+            shape((slots - early,) + jacobian.shape[1:], bf16),
+        ),
+        [SMEM()] * 2 + [VMEM()] * 9 + [HBM()],
         dot_flops,
         2 * jacobian.size,
-        [pltpu.VMEM((2 * cols * species, probes, width), bf16), pltpu.VMEM((probes, width), f32)],
-    )(crossing, live, rows, across, within, from_across, from_within, faced, norm, curved, jac)
+        [
+            pltpu.VMEM((2 * cols * species, probes, width), bf16),
+            pltpu.VMEM((probes, width), f32),
+            pltpu.SemaphoreType.DMA,
+        ],
+    )(
+        crossing, live, rows, across, within, from_across, from_within, faced, norm, curved, jac,
+        in_hbm(jacobian),
+    )
     near_step, *far_steps = sum_steps(devices)
     held = [sums] + partners(sums, near_step)
 
     image, across, within = call(
         backward_kernel,
         (whole, near, near),
-        [SMEM()] * 3 + [VMEM()] * 6,
+        [SMEM()] * 3 + [VMEM()] * 7,
         dot_flops,
         2 * jacobian.size,
         [
             pltpu.VMEM((2 * cols * species, probes, width), f32),
             pltpu.VMEM((2, rim) + column, f32),
         ],
-    )(crossing, length_class, live, smooth_weight, weighted, jac, begun, from_across, from_within)
+    )(crossing, length_class, live, smooth_weight, weighted, jac, late, begun, from_across, from_within)
     from_across = swapped_across(across)
     within, *held = lax.optimization_barrier((within, *held))
     sums = tree_sum(held)
@@ -376,6 +411,8 @@
         [VMEM()] * (6 + len(held)),
         8 * elements,
         28 * elements,
+        [pltpu.VMEM(direction.shape, f32)] * 2 + [pltpu.SemaphoreType.DMA((2,))],
+        [HBM()] * 2 + [VMEM()],
     )(solution, residual, direction, image, from_across, from_within, *held)
     return solution_next, residual_next, step_length.reshape(probes)
 

time: 26.5 us -> 27 us (1.019); the launches traced: 26.8 us -> 26.7 us
  waiting for transfers between devices: 5.55 us -> 5.1 us
    pallas_call x1, Pallas kernels: 1.24 us -> 1.74 us  [local(): call(final_kernel, (whole, whole, shape((1, probes), f32)), [VMEM()] * (6...]
    pallas_call x1, Pallas kernels: 3.11 us -> 2.63 us  [local(): call(inner_kernel, (shape((2 * cols,) + column, f32), shape((2, rim) + co...]
    ppermute x5, waiting for transfers between devices: 5.54 us -> 5.09 us  [partners(): lax.ppermute(array, 'orbit', [(i, i ^ mask) for i in devices])]
    ppermute x5, starting transfers between devices: 2.77 us -> 3.12 us  [partners(): lax.ppermute(array, 'orbit', [(i, i ^ mask) for i in devices])]
  transfers between devices with their start and end apart: 9 -> 9, of which waited for: 3 -> 4; matrix products, arithmetic and copies ran while one was open for 0% -> 0% of each run, Pallas kernels for 18% -> 17%
where the time goes in v3:
time: 27 us; the launch traced here: 26.7 us
  starting transfers between devices  10.6 us (39%)
  Pallas kernels  9.61 us (36%)
  waiting for transfers between devices  5.1 us (19%)
  between operations  1.42 us (5%)
    ppermute x2, starting transfers between devices, swapped_across(): lax.ppermute(half, 'orbit', [(i, (i + 2 * (i % 2) - 1) % count) for i in...  7.44 us
    ppermute x5, waiting for transfers between devices, partners(): lax.ppermute(array, 'orbit', [(i, i ^ mask) for i in devices])  5.09 us
    ppermute x5, starting transfers between devices, partners(): lax.ppermute(array, 'orbit', [(i, i ^ mask) for i in devices])  3.12 us
    pallas_call x1, Pallas kernels, local(): call(inner_kernel, (shape((2 * cols,) + column, f32), shape((2, rim) + co...  2.63 us
    pallas_call x1, Pallas kernels, local(): call(forward_kernel, (shape((slots, probes, width), bf16), shape((probes...  2.36 us
    pallas_call x1, Pallas kernels, local(): call(backward_kernel, (whole, near, near), [SMEM()] * 3 + [VMEM()] * 7, d...  1.8 us
    pallas_call x1, Pallas kernels, local(): call(final_kernel, (whole, whole, shape((1, probes), f32)), [VMEM()] * (6...  1.74 us
    pallas_call x1, Pallas kernels, local(): call(rounding_kernel, (whole, near, near), [HBM()], 2 * elements, 10 * el...  1.07 us
  transfers between devices with their start and end apart: 9, of which 4 were waited for; matrix products, arithmetic and copies ran while one was open for 0% of the time, Pallas kernels for 17%

profile of v3, /device:TPU:0, one launch (start us, length us, event | category | flops | bytes accessed | tf_op | source)
XLA Modules:
  0.0 26.7 jit_solution(14984865447213981418)
XLA Ops:
  0.6 1.1 %shard_map.112 = (f32[8,8,16,128]{3,2,1,0:T(8,128)S(1)}, bf16[4,8,16,128]{3,2,1,0:T(8,128)(2,1)S(1)}, bf16[4,8,16,128]{3,2,1,0:T(8,128)(2,1)S(1)}) custom-call(f32[8,8,16,128]{3,2,1,0:T(8,128)} %direction.1), custom_call_target="tpu_custom_call" | custom-call | flops 262144 | bytes 1310720 | tf_op jit(solution)/shard_map/pallas_call | solution.py:329
  1.7 5.5 %collective-permute-start = (bf16[4,8,16,128]{3,2,1,0:T(8,128)(2,1)S(1)}, bf16[4,8,16,128]{3,2,1,0:T(8,128)(2,1)S(1)}, u32[]{:S(2)}, u32[]{:S(2)}) collective-permute-start(bf16[4,8,16,128]{3,2,1,0:T(8,128)(2,1)S(1)} %get-tuple-element.35.across), channel_id=1, source_target_pairs={{0,15},{1,2},{2,1},{3,4},{4,3},{5,6},{6,5},{7,8},{8,7},{9,10},{10,... | collective-permute-start | bytes 393224 | tf_op jit(solution)/shard_map/ppermute | solution.py:284
  7.2 0.0 collective-permute-start.1
  7.9 2.6 %shard_map.113 = (f32[16,8,16,128]{3,2,1,0:T(8,128)S(1)}, f32[2,4,8,16,128]{4,3,2,1,0:T(8,128)S(1)}, f32[16,128]{1,0:T(8,128)S(1)}, f32[16,128]{1,0:T(8,128)S(1)...) custom-call(f32[8,8,16,128]{3,2,1,0:T(8,128)S(1)} %get-tuple-element, ...), custom_call_target="tpu_custom_call" | custom-call | flops 7864320 | bytes 12582912 | tf_op jit(solution)/shard_map/pallas_call | solution.py:339
  10.5 0.0 collective-permute-done.from_across
  10.5 0.0 collective-permute-done.1.from_within
  10.5 0.0 copy-start.3
  10.5 2.4 %shard_map.114 = (bf16[8,16,128]{2,1,0:T(8,128)(2,1)S(1)}, f32[8,128]{1,0:T(8,128)S(1)}, bf16[2,24,128,128]{3,2,1,0:T(8,128)(2,1)S(1)}) custom-call(s32[8,24]{1,0:T(8,128)S(4)} %get-tuple-element.31.crossing, s32[8]{0:T(128)S(4)} %get-tuple-element.33.live, f32[8,128]{1,0:T(8,128)S(1)} %get-tuple-element.34.rows, ...), custom_call_target="tpu_custom_call" | custom-call | flops 100663296 | bytes 6291456 | tf_op jit(solution)/shard_map/pallas_call | solution.py:366
  12.9 0.0 copy-start
  12.9 0.0 copy-start.1
  12.9 0.0 copy-start.2
  13.0 0.1 collective-permute-start.3
  13.0 0.0 copy-done.3
  13.0 1.8 %shard_map.115 = (f32[8,8,16,128]{3,2,1,0:T(8,128)S(1)}, bf16[4,8,16,128]{3,2,1,0:T(8,128)(2,1)S(1)}, bf16[4,8,16,128]{3,2,1,0:T(8,128)(2,1)S(1)}) custom-call(s32[8,24]{1,0:T(8,128)S(4)} %get-tuple-element.31.crossing, s32[128]{0:T(128)S(4)} %get-tuple-element.32.classes, s32[8]{0:T(128)S(4)} %get-tuple-element.33.live, f32[8,128]{1,0:T(8,128)S(1)} %copy-done.3, ...), custom_call_target="tpu_custom_call" | custom-call | flops 100663296 | bytes 6291456 | tf_op jit(solution)/shard_map/pallas_call | solution.py:387
  14.8 1.8 %collective-permute-done.3 = f32[8,128]{1,0:T(8,128)S(1)} collective-permute-done((f32[8,128]{1,0:T(8,128)S(1)}, f32[8,128]{1,0:T(8,128)S(1)}, u32[]{:S(2)}, u32[]{:S(2)}) %collective-permute-start.3) | collective-permute-done | bytes 4128 | tf_op jit(solution)/shard_map/ppermute | solution.py:300
  16.6 0.0 collective-permute-start.4
  16.6 1.9 %collective-permute-start.2 = (bf16[4,8,16,128]{3,2,1,0:T(8,128)(2,1)S(1)}, bf16[4,8,16,128]{3,2,1,0:T(8,128)(2,1)S(1)}, u32[]{:S(2)}, u32[]{:S(2)}) collective-permute-start(bf16[4,8,16,128]{3,2,1,0:T(8,128)(2,1)S(1)} %get-tuple-element.45), channel_id=1, source_target_pairs={{0,15},{1,2},{2,1},{3,4},{4,3},{5,6},{6,5},{7,8},{8,7},{9,10},{10,... | collective-permute-start | bytes 393224 | tf_op jit(solution)/shard_map/ppermute | solution.py:284
  18.6 1.7 %collective-permute-done.4 = f32[8,128]{1,0:T(8,128)S(1)} collective-permute-done((f32[8,128]{1,0:T(8,128)S(1)}, f32[8,128]{1,0:T(8,128)S(1)}, u32[]{:S(2)}, u32[]{:S(2)}) %collective-permute-start.4) | collective-permute-done | bytes 4128 | tf_op jit(solution)/shard_map/ppermute | solution.py:300
  20.2 0.0 collective-permute-start.5
  20.2 0.0 collective-permute-start.8
  20.3 3.0 %collective-permute-start.7 = (f32[8,128]{1,0:T(8,128)S(1)}, f32[8,128]{1,0:T(8,128)S(1)}, u32[]{:S(2)}, u32[]{:S(2)}) collective-permute-start(f32[8,128]{1,0:T(8,128)S(1)} %add.7.rest_0_), channel_id=1, source_target_pairs={{0,8},{1,9},{2,10},{3,11},{4,12},{5,13},{6,14},{7,15},{8,0},{9,1},... | collective-permute-start | bytes 12296 | tf_op jit(solution)/shard_map/ppermute | solution.py:300
  23.3 0.0 collective-permute-start.6
  23.3 0.9 %collective-permute-done.8.rest_3_ = f32[8,128]{1,0:T(8,128)S(1)} collective-permute-done((f32[8,128]{1,0:T(8,128)S(1)}, f32[8,128]{1,0:T(8,128)S(1)}, u32[]{:S(2)}, u32[]{:S(2)}) %collective-permute-start.8) | collective-permute-done | bytes 4128 | tf_op jit(solution)/shard_map/ppermute | solution.py:300
  24.2 0.8 %collective-permute-done.7.rest_2_ = f32[8,128]{1,0:T(8,128)S(1)} collective-permute-done((f32[8,128]{1,0:T(8,128)S(1)}, f32[8,128]{1,0:T(8,128)S(1)}, u32[]{:S(2)}, u32[]{:S(2)}) %collective-permute-start.7) | collective-permute-done | bytes 4128 | tf_op jit(solution)/shard_map/ppermute | solution.py:300
  24.9 0.0 collective-permute-done.6.rest_1_
  24.9 0.0 collective-permute-done.2.from_across
  24.9 0.0 collective-permute-done.5.from_within
  24.9 0.0 copy-done
  25.0 0.0 copy-done.1
  25.0 0.0 copy-done.2
  25.0 1.7 %shard_map.116 = (f32[8,8,16,128]{3,2,1,0:T(8,128)}, f32[8,8,16,128]{3,2,1,0:T(8,128)}, f32[1,16]{1,0:T(1,128)}) custom-call(f32[8,8,16,128]{3,2,1,0:T(8,128)S(1)} %copy-done.2, f32[8,8,16,128]{3,2,1,0:T(8,128)S(1)} %copy-done.1, f32[8,8,16,128]{3,2,1,0:T(8,128)S(1)} %copy-done, f32[8,8,16,128]{3,2,1,0:T(8,128)S(1)} %get-tuple-element.44.image, ...), custom_call_target="tpu_custom_call" | custom-call | flops 1048576 | bytes 3670016 | tf_op jit(solution)/shard_map/pallas_call | solution.py:408
  (2 shorter events, 0.0 us)
Async XLA Ops:
  1.7 8.8 %collective-permute-start = (bf16[4,8,16,128]{3,2,1,0:T(8,128)(2,1)S(1)}, bf16[4,8,16,128]{3,2,1,0:T(8,128)(2,1)S(1)}, u32[]{:S(2)}, u32[]{:S(2)}) collective-permute-start(bf16[4,8,16,128]{3,2,1,0:T(8,128)(2,1)S(1)} %get-tuple-element.35.across), channel_id=1, source_target_pairs={{0,15},{1,2},{2,1},{3,4},{4,3},{5,6},{6,5},{7,8},{8,7},{9,10},{10,... | collective-permute-start | bytes 393224 | tf_op jit(solution)/shard_map/ppermute | solution.py:284
  7.2 3.3 %collective-permute-start.1 = (bf16[4,8,16,128]{3,2,1,0:T(8,128)(2,1)S(1)}, bf16[4,8,16,128]{3,2,1,0:T(8,128)(2,1)S(1)}, u32[]{:S(2)}, u32[]{:S(2)}) collective-permute-start(bf16[4,8,16,128]{3,2,1,0:T(8,128)(2,1)S(1)} %get-tuple-element.36.within), channel_id=1, source_target_pairs={{0,1},{1,0},{2,3},{3,2},{4,5},{5,4},{6,7},{7,6},{8,9},{9,8},{10,11... | collective-permute-start | bytes 393224 | tf_op jit(solution)/shard_map/ppermute | solution.py:288
  10.5 2.5 %copy-start.3 = (f32[8,128]{1,0:T(8,128)S(1)}, f32[8,128]{1,0:T(8,128)}, u32[]{:S(2)}) copy-start(f32[8,128]{1,0:T(8,128)} %smooth.1) | copy-start | bytes 12292
  12.9 12.0 %copy-start = (f32[8,8,16,128]{3,2,1,0:T(8,128)S(1)}, f32[8,8,16,128]{3,2,1,0:T(8,128)}, u32[]{:S(2)}) copy-start(f32[8,8,16,128]{3,2,1,0:T(8,128)} %direction.1) | copy-start | bytes 1572868
  12.9 12.0 %copy-start.1 = (f32[8,8,16,128]{3,2,1,0:T(8,128)S(1)}, f32[8,8,16,128]{3,2,1,0:T(8,128)}, u32[]{:S(2)}) copy-start(f32[8,8,16,128]{3,2,1,0:T(8,128)} %residual.1) | copy-start | bytes 1572868
  12.9 12.0 %copy-start.2 = (f32[8,8,16,128]{3,2,1,0:T(8,128)S(1)}, f32[8,8,16,128]{3,2,1,0:T(8,128)}, u32[]{:S(2)}) copy-start(f32[8,8,16,128]{3,2,1,0:T(8,128)} %solution.1) | copy-start | bytes 1572868
  13.0 3.7 %collective-permute-start.3 = (f32[8,128]{1,0:T(8,128)S(1)}, f32[8,128]{1,0:T(8,128)S(1)}, u32[]{:S(2)}, u32[]{:S(2)}) collective-permute-start(f32[8,128]{1,0:T(8,128)S(1)} %get-tuple-element.49), channel_id=1, source_target_pairs={{0,2},{1,3},{2,0},{3,1},{4,6},{5,7},{6,4},{7,5},{8,10},{9,11},{10,... | collective-permute-start | bytes 12296 | tf_op jit(solution)/shard_map/ppermute | solution.py:300
  16.6 3.6 %collective-permute-start.4 = (f32[8,128]{1,0:T(8,128)S(1)}, f32[8,128]{1,0:T(8,128)S(1)}, u32[]{:S(2)}, u32[]{:S(2)}) collective-permute-start(f32[8,128]{1,0:T(8,128)S(1)} %add.6), channel_id=1, source_target_pairs={{0,4},{1,5},{2,6},{3,7},{4,0},{5,1},{6,2},{7,3},{8,12},{9,13},{10,... | collective-permute-start | bytes 12296 | tf_op jit(solution)/shard_map/ppermute | solution.py:300
  16.6 8.3 %collective-permute-start.2 = (bf16[4,8,16,128]{3,2,1,0:T(8,128)(2,1)S(1)}, bf16[4,8,16,128]{3,2,1,0:T(8,128)(2,1)S(1)}, u32[]{:S(2)}, u32[]{:S(2)}) collective-permute-start(bf16[4,8,16,128]{3,2,1,0:T(8,128)(2,1)S(1)} %get-tuple-element.45), channel_id=1, source_target_pairs={{0,15},{1,2},{2,1},{3,4},{4,3},{5,6},{6,5},{7,8},{8,7},{9,10},{10,... | collective-permute-start | bytes 393224 | tf_op jit(solution)/shard_map/ppermute | solution.py:284
  20.2 4.7 %collective-permute-start.5 = (bf16[4,8,16,128]{3,2,1,0:T(8,128)(2,1)S(1)}, bf16[4,8,16,128]{3,2,1,0:T(8,128)(2,1)S(1)}, u32[]{:S(2)}, u32[]{:S(2)}) collective-permute-start(bf16[4,8,16,128]{3,2,1,0:T(8,128)(2,1)S(1)} %get-tuple-element.51), channel_id=1, source_target_pairs={{0,1},{1,0},{2,3},{3,2},{4,5},{5,4},{6,7},{7,6},{8,9},{9,8},{10,11... | collective-permute-start | bytes 393224 | tf_op jit(solution)/shard_map/ppermute | solution.py:288
  20.2 3.9 %collective-permute-start.8 = (f32[8,128]{1,0:T(8,128)S(1)}, f32[8,128]{1,0:T(8,128)S(1)}, u32[]{:S(2)}, u32[]{:S(2)}) collective-permute-start(f32[8,128]{1,0:T(8,128)S(1)} %add.7.rest_0_), channel_id=1, source_target_pairs={{0,9},{1,8},{2,11},{3,10},{4,13},{5,12},{6,15},{7,14},{8,1},{9,0},... | collective-permute-start | bytes 12296 | tf_op jit(solution)/shard_map/ppermute | solution.py:300
  20.3 4.7 %collective-permute-start.7 = (f32[8,128]{1,0:T(8,128)S(1)}, f32[8,128]{1,0:T(8,128)S(1)}, u32[]{:S(2)}, u32[]{:S(2)}) collective-permute-start(f32[8,128]{1,0:T(8,128)S(1)} %add.7.rest_0_), channel_id=1, source_target_pairs={{0,8},{1,9},{2,10},{3,11},{4,12},{5,13},{6,14},{7,15},{8,0},{9,1},... | collective-permute-start | bytes 12296 | tf_op jit(solution)/shard_map/ppermute | solution.py:300
  23.3 1.6 %collective-permute-start.6 = (f32[8,128]{1,0:T(8,128)S(1)}, f32[8,128]{1,0:T(8,128)S(1)}, u32[]{:S(2)}, u32[]{:S(2)}) collective-permute-start(f32[8,128]{1,0:T(8,128)S(1)} %add.7.rest_0_), channel_id=1, source_target_pairs={{0,1},{1,0},{2,3},{3,2},{4,5},{5,4},{6,7},{7,6},{8,9},{9,8},{10,11... | collective-permute-start | bytes 12296 | tf_op jit(solution)/shard_map/ppermute | solution.py:300

commit v4 on v3

--- a/solution.py
+++ b/solution.py
@@ -252,7 +252,7 @@
 def final_kernel(
     solution, residual, direction, image, from_across, from_within, *rest
 ):
-    *held, solution_out, residual_out, step_length, solution_next, residual_next, sems = rest
+    *held, solution_next, residual_next, step_length = rest
     whole = tree_sum([part[...] for part in held])
     norm = jnp.concatenate([whole[:, 0:1], whole[:, 2:3]], axis=0)
     curvature = jnp.concatenate([whole[:, 1:2], whole[:, 3:4]], axis=0)
@@ -262,20 +262,11 @@
     step_length[...] = jnp.transpose(wide)[0:1]
     wide = wide[None]
     odd = parity()
-    copies = [
-        pltpu.make_async_copy(solution_next, solution_out, sems.at[0]),
-        pltpu.make_async_copy(residual_next, residual_out, sems.at[1]),
-    ]
-    for c in range(2 * rim):
-        solution_next[c] = masked(solution[c] + wide * direction[c])
-    copies[0].start()
     for q in range(rim):
         for c, part in (odd * rim + q, from_across), ((1 - odd) * rim + q, from_within):
             total = masked(image[c] + part[q].astype(jnp.float32))
+            solution_next[c] = masked(solution[c] + wide * direction[c])
             residual_next[c] = masked(residual[c]) - wide * total
-    copies[1].start()
-    for copy in copies:
-        copy.wait()
 
 
 def swapped_across(half):
@@ -289,8 +280,8 @@
 
 
 def sum_steps(devices):
-    assert devices >= 8 and devices & (devices - 1) == 0
-    return [[1 << b] for b in range(1, devices.bit_length() - 2)] + [[1, devices // 2]]
+    assert devices >= 4 and devices & (devices - 1) == 0
+    return [[1 << b] for b in range(1, devices.bit_length() - 1)] + [[1]]
 
 
 def partners(array, bits):
@@ -411,8 +402,6 @@
         [VMEM()] * (6 + len(held)),
         8 * elements,
         28 * elements,
-        [pltpu.VMEM(direction.shape, f32)] * 2 + [pltpu.SemaphoreType.DMA((2,))],
-        [HBM()] * 2 + [VMEM()],
     )(solution, residual, direction, image, from_across, from_within, *held)
     return solution_next, residual_next, step_length.reshape(probes)
 

time: 27 us -> 26.1 us (0.967); the launches traced: 26.7 us -> 26.3 us
  Pallas kernels: 9.61 us -> 6.72 us
  waiting for transfers between devices: 5.1 us -> 7.07 us
  starting transfers between devices: 10.6 us -> 11 us
    ppermute x5 -> x4, waiting for transfers between devices: 5.09 us -> 7.06 us  [partners(): lax.ppermute(array, 'orbit', [(i, i ^ mask) for i in devices])]
    ppermute x2, starting transfers between devices: 7.44 us -> 9.27 us  [swapped_across(): lax.ppermute(half, 'orbit', [(i, (i + 2 * (i % 2) - 1) % count) for i in...]
    ppermute x5 -> x4, starting transfers between devices: 3.12 us -> 1.76 us  [partners(): lax.ppermute(array, 'orbit', [(i, i ^ mask) for i in devices])]
    pallas_call x1, Pallas kernels: 2.36 us -> 1.14 us  [local(): call(forward_kernel, (shape((slots, probes, width), bf16), shape((probes...]
    pallas_call x1, Pallas kernels: 1.8 us -> 1.12 us  [local(): call(backward_kernel, (whole, near, near), [SMEM()] * 3 + [VMEM()] * 7, d...]
    pallas_call x1, Pallas kernels: 1.74 us -> 1.23 us  [local(): call(final_kernel, (whole, whole, shape((1, probes), f32)), [VMEM()] * (6...]
    pallas_call x1, Pallas kernels: 2.63 us -> 2.16 us  [local(): call(inner_kernel, (shape((2 * cols,) + column, f32), shape((2, rim) + co...]
  transfers between devices with their start and end apart: 9 -> 8, of which waited for: 4 -> 3; matrix products, arithmetic and copies ran while one was open for 0% -> 0% of each run, Pallas kernels for 17% -> 12%
where the time goes in v4:
time: 26.1 us; the launch traced here: 26.3 us
  starting transfers between devices  11 us (42%)
  waiting for transfers between devices  7.07 us (27%)
  Pallas kernels  6.72 us (26%)
  between operations  1.41 us (5%)
    ppermute x2, starting transfers between devices, swapped_across(): lax.ppermute(half, 'orbit', [(i, (i + 2 * (i % 2) - 1) % count) for i in...  9.27 us
    ppermute x4, waiting for transfers between devices, partners(): lax.ppermute(array, 'orbit', [(i, i ^ mask) for i in devices])  7.06 us
    pallas_call x1, Pallas kernels, local(): call(inner_kernel, (shape((2 * cols,) + column, f32), shape((2, rim) + co...  2.16 us
    ppermute x4, starting transfers between devices, partners(): lax.ppermute(array, 'orbit', [(i, i ^ mask) for i in devices])  1.76 us
    pallas_call x1, Pallas kernels, local(): call(final_kernel, (whole, whole, shape((1, probes), f32)), [VMEM()] * (6...  1.23 us
    pallas_call x1, Pallas kernels, local(): call(forward_kernel, (shape((slots, probes, width), bf16), shape((probes...  1.14 us
    pallas_call x1, Pallas kernels, local(): call(backward_kernel, (whole, near, near), [SMEM()] * 3 + [VMEM()] * 7, d...  1.12 us
    pallas_call x1, Pallas kernels, local(): call(rounding_kernel, (whole, near, near), [HBM()], 2 * elements, 10 * el...  1.07 us
  transfers between devices with their start and end apart: 8, of which 3 were waited for; matrix products, arithmetic and copies ran while one was open for 0% of the time, Pallas kernels for 12%

profile of v4, /device:TPU:0, one launch (start us, length us, event | category | flops | bytes accessed | tf_op | source)
XLA Modules:
  0.0 26.3 jit_solution(9023828758286519735)
XLA Ops:
  0.6 1.1 %shard_map.112 = (f32[8,8,16,128]{3,2,1,0:T(8,128)S(1)}, bf16[4,8,16,128]{3,2,1,0:T(8,128)(2,1)S(1)}, bf16[4,8,16,128]{3,2,1,0:T(8,128)(2,1)S(1)}) custom-call(f32[8,8,16,128]{3,2,1,0:T(8,128)} %direction.1), custom_call_target="tpu_custom_call" | custom-call | flops 262144 | bytes 1310720 | tf_op jit(solution)/shard_map/pallas_call | solution.py:320
  1.7 5.5 %collective-permute-start = (bf16[4,8,16,128]{3,2,1,0:T(8,128)(2,1)S(1)}, bf16[4,8,16,128]{3,2,1,0:T(8,128)(2,1)S(1)}, u32[]{:S(2)}, u32[]{:S(2)}) collective-permute-start(bf16[4,8,16,128]{3,2,1,0:T(8,128)(2,1)S(1)} %get-tuple-element.35.across), channel_id=1, source_target_pairs={{0,15},{1,2},{2,1},{3,4},{4,3},{5,6},{6,5},{7,8},{8,7},{9,10},{10,... | collective-permute-start | bytes 393224 | tf_op jit(solution)/shard_map/ppermute | solution.py:275
  7.2 0.0 collective-permute-start.1
  7.9 2.2 %shard_map.113 = (f32[16,8,16,128]{3,2,1,0:T(8,128)S(1)}, f32[2,4,8,16,128]{4,3,2,1,0:T(8,128)S(1)}, f32[16,128]{1,0:T(8,128)S(1)}, f32[16,128]{1,0:T(8,128)S(1)...) custom-call(f32[8,8,16,128]{3,2,1,0:T(8,128)S(1)} %get-tuple-element, ...), custom_call_target="tpu_custom_call" | custom-call | flops 7864320 | bytes 12582912 | tf_op jit(solution)/shard_map/pallas_call | solution.py:330
  10.0 0.0 collective-permute-done.from_across
  10.1 0.0 collective-permute-done.1.from_within
  10.1 0.0 copy-start.3
  10.1 1.1 %shard_map.114 = (bf16[8,16,128]{2,1,0:T(8,128)(2,1)S(1)}, f32[8,128]{1,0:T(8,128)S(1)}, bf16[2,24,128,128]{3,2,1,0:T(8,128)(2,1)S(1)}) custom-call(s32[8,24]{1,0:T(8,128)S(4)} %get-tuple-element.31.crossing, s32[8]{0:T(128)S(4)} %get-tuple-element.33.live, f32[8,128]{1,0:T(8,128)S(1)} %get-tuple-element.34.rows, ...), custom_call_target="tpu_custom_call" | custom-call | flops 100663296 | bytes 6291456 | tf_op jit(solution)/shard_map/pallas_call | solution.py:357
  11.2 0.0 copy-start
  11.2 0.0 copy-start.1
  11.2 0.0 copy-start.2
  11.3 0.1 collective-permute-start.3
  11.3 0.0 copy-done.3
  11.3 1.1 %shard_map.115 = (f32[8,8,16,128]{3,2,1,0:T(8,128)S(1)}, bf16[4,8,16,128]{3,2,1,0:T(8,128)(2,1)S(1)}, bf16[4,8,16,128]{3,2,1,0:T(8,128)(2,1)S(1)}) custom-call(s32[8,24]{1,0:T(8,128)S(4)} %get-tuple-element.31.crossing, s32[128]{0:T(128)S(4)} %get-tuple-element.32.classes, s32[8]{0:T(128)S(4)} %get-tuple-element.33.live, f32[8,128]{1,0:T(8,128)S(1)} %copy-done.3, ...), custom_call_target="tpu_custom_call" | custom-call | flops 100663296 | bytes 6291456 | tf_op jit(solution)/shard_map/pallas_call | solution.py:378
  12.5 2.5 %collective-permute-done.3 = f32[8,128]{1,0:T(8,128)S(1)} collective-permute-done((f32[8,128]{1,0:T(8,128)S(1)}, f32[8,128]{1,0:T(8,128)S(1)}, u32[]{:S(2)}, u32[]{:S(2)}) %collective-permute-start.3) | collective-permute-done | bytes 4128 | tf_op jit(solution)/shard_map/ppermute | solution.py:291
  14.9 0.6 %collective-permute-start.4 = (f32[8,128]{1,0:T(8,128)S(1)}, f32[8,128]{1,0:T(8,128)S(1)}, u32[]{:S(2)}, u32[]{:S(2)}) collective-permute-start(f32[8,128]{1,0:T(8,128)S(1)} %add.9), channel_id=1, source_target_pairs={{0,4},{1,5},{2,6},{3,7},{4,0},{5,1},{6,2},{7,3},{8,12},{9,13},{10,... | collective-permute-start | bytes 12296 | tf_op jit(solution)/shard_map/ppermute | solution.py:291
  15.5 3.8 %collective-permute-start.2 = (bf16[4,8,16,128]{3,2,1,0:T(8,128)(2,1)S(1)}, bf16[4,8,16,128]{3,2,1,0:T(8,128)(2,1)S(1)}, u32[]{:S(2)}, u32[]{:S(2)}) collective-permute-start(bf16[4,8,16,128]{3,2,1,0:T(8,128)(2,1)S(1)} %get-tuple-element.45), channel_id=1, source_target_pairs={{0,15},{1,2},{2,1},{3,4},{4,3},{5,6},{6,5},{7,8},{8,7},{9,10},{10,... | collective-permute-start | bytes 393224 | tf_op jit(solution)/shard_map/ppermute | solution.py:275
  19.3 0.0 collective-permute-done.4
  19.3 0.0 collective-permute-start.5
  19.3 1.1 %collective-permute-start.6 = (f32[8,128]{1,0:T(8,128)S(1)}, f32[8,128]{1,0:T(8,128)S(1)}, u32[]{:S(2)}, u32[]{:S(2)}) collective-permute-start(f32[8,128]{1,0:T(8,128)S(1)} %add.10), channel_id=1, source_target_pairs={{0,8},{1,9},{2,10},{3,11},{4,12},{5,13},{6,14},{7,15},{8,0},{9,1},... | collective-permute-start | bytes 12296 | tf_op jit(solution)/shard_map/ppermute | solution.py:291
  20.4 3.4 %collective-permute-done.6 = f32[8,128]{1,0:T(8,128)S(1)} collective-permute-done((f32[8,128]{1,0:T(8,128)S(1)}, f32[8,128]{1,0:T(8,128)S(1)}, u32[]{:S(2)}, u32[]{:S(2)}) %collective-permute-start.6) | collective-permute-done | bytes 4128 | tf_op jit(solution)/shard_map/ppermute | solution.py:291
  23.8 0.0 collective-permute-start.7
  23.8 1.2 %collective-permute-done.7.rest_1_ = f32[8,128]{1,0:T(8,128)S(1)} collective-permute-done((f32[8,128]{1,0:T(8,128)S(1)}, f32[8,128]{1,0:T(8,128)S(1)}, u32[]{:S(2)}, u32[]{:S(2)}) %collective-permute-start.7) | collective-permute-done | bytes 4128 | tf_op jit(solution)/shard_map/ppermute | solution.py:291
  25.0 0.0 collective-permute-done.2.from_across
  25.0 0.0 collective-permute-done.5.from_within
  25.0 0.0 copy-done
  25.0 0.0 copy-done.1
  25.0 0.0 copy-done.2
  25.0 1.2 %shard_map.116 = (f32[8,8,16,128]{3,2,1,0:T(8,128)}, f32[8,8,16,128]{3,2,1,0:T(8,128)}, f32[1,16]{1,0:T(1,128)}) custom-call(f32[8,8,16,128]{3,2,1,0:T(8,128)S(1)} %copy-done.2, f32[8,8,16,128]{3,2,1,0:T(8,128)S(1)} %copy-done.1, f32[8,8,16,128]{3,2,1,0:T(8,128)S(1)} %copy-done, f32[8,8,16,128]{3,2,1,0:T(8,128)S(1)} %get-tuple-element.44.image, ...), custom_call_target="tpu_custom_call" | custom-call | flops 1048576 | bytes 3670016 | tf_op jit(solution)/shard_map/pallas_call | solution.py:399
  (3 shorter events, 0.0 us)
Async XLA Ops:
  1.7 8.3 %collective-permute-start = (bf16[4,8,16,128]{3,2,1,0:T(8,128)(2,1)S(1)}, bf16[4,8,16,128]{3,2,1,0:T(8,128)(2,1)S(1)}, u32[]{:S(2)}, u32[]{:S(2)}) collective-permute-start(bf16[4,8,16,128]{3,2,1,0:T(8,128)(2,1)S(1)} %get-tuple-element.35.across), channel_id=1, source_target_pairs={{0,15},{1,2},{2,1},{3,4},{4,3},{5,6},{6,5},{7,8},{8,7},{9,10},{10,... | collective-permute-start | bytes 393224 | tf_op jit(solution)/shard_map/ppermute | solution.py:275
  7.2 2.8 %collective-permute-start.1 = (bf16[4,8,16,128]{3,2,1,0:T(8,128)(2,1)S(1)}, bf16[4,8,16,128]{3,2,1,0:T(8,128)(2,1)S(1)}, u32[]{:S(2)}, u32[]{:S(2)}) collective-permute-start(bf16[4,8,16,128]{3,2,1,0:T(8,128)(2,1)S(1)} %get-tuple-element.36.within), channel_id=1, source_target_pairs={{0,1},{1,0},{2,3},{3,2},{4,5},{5,4},{6,7},{7,6},{8,9},{9,8},{10,11... | collective-permute-start | bytes 393224 | tf_op jit(solution)/shard_map/ppermute | solution.py:279
  10.1 1.3 %copy-start.3 = (f32[8,128]{1,0:T(8,128)S(1)}, f32[8,128]{1,0:T(8,128)}, u32[]{:S(2)}) copy-start(f32[8,128]{1,0:T(8,128)} %smooth.1) | copy-start | bytes 12292
  11.2 13.8 %copy-start = (f32[8,8,16,128]{3,2,1,0:T(8,128)S(1)}, f32[8,8,16,128]{3,2,1,0:T(8,128)}, u32[]{:S(2)}) copy-start(f32[8,8,16,128]{3,2,1,0:T(8,128)} %direction.1) | copy-start | bytes 1572868
  11.2 13.8 %copy-start.1 = (f32[8,8,16,128]{3,2,1,0:T(8,128)S(1)}, f32[8,8,16,128]{3,2,1,0:T(8,128)}, u32[]{:S(2)}) copy-start(f32[8,8,16,128]{3,2,1,0:T(8,128)} %residual.1) | copy-start | bytes 1572868
  11.2 13.8 %copy-start.2 = (f32[8,8,16,128]{3,2,1,0:T(8,128)S(1)}, f32[8,8,16,128]{3,2,1,0:T(8,128)}, u32[]{:S(2)}) copy-start(f32[8,8,16,128]{3,2,1,0:T(8,128)} %solution.1) | copy-start | bytes 1572868
  11.3 3.7 %collective-permute-start.3 = (f32[8,128]{1,0:T(8,128)S(1)}, f32[8,128]{1,0:T(8,128)S(1)}, u32[]{:S(2)}, u32[]{:S(2)}) collective-permute-start(f32[8,128]{1,0:T(8,128)S(1)} %get-tuple-element.49), channel_id=1, source_target_pairs={{0,2},{1,3},{2,0},{3,1},{4,6},{5,7},{6,4},{7,5},{8,10},{9,11},{10,... | collective-permute-start | bytes 12296 | tf_op jit(solution)/shard_map/ppermute | solution.py:291
  14.9 4.3 %collective-permute-start.4 = (f32[8,128]{1,0:T(8,128)S(1)}, f32[8,128]{1,0:T(8,128)S(1)}, u32[]{:S(2)}, u32[]{:S(2)}) collective-permute-start(f32[8,128]{1,0:T(8,128)S(1)} %add.9), channel_id=1, source_target_pairs={{0,4},{1,5},{2,6},{3,7},{4,0},{5,1},{6,2},{7,3},{8,12},{9,13},{10,... | collective-permute-start | bytes 12296 | tf_op jit(solution)/shard_map/ppermute | solution.py:291
  15.5 9.5 %collective-permute-start.2 = (bf16[4,8,16,128]{3,2,1,0:T(8,128)(2,1)S(1)}, bf16[4,8,16,128]{3,2,1,0:T(8,128)(2,1)S(1)}, u32[]{:S(2)}, u32[]{:S(2)}) collective-permute-start(bf16[4,8,16,128]{3,2,1,0:T(8,128)(2,1)S(1)} %get-tuple-element.45), channel_id=1, source_target_pairs={{0,15},{1,2},{2,1},{3,4},{4,3},{5,6},{6,5},{7,8},{8,7},{9,10},{10,... | collective-permute-start | bytes 393224 | tf_op jit(solution)/shard_map/ppermute | solution.py:275
  19.3 5.8 %collective-permute-start.5 = (bf16[4,8,16,128]{3,2,1,0:T(8,128)(2,1)S(1)}, bf16[4,8,16,128]{3,2,1,0:T(8,128)(2,1)S(1)}, u32[]{:S(2)}, u32[]{:S(2)}) collective-permute-start(bf16[4,8,16,128]{3,2,1,0:T(8,128)(2,1)S(1)} %get-tuple-element.51), channel_id=1, source_target_pairs={{0,1},{1,0},{2,3},{3,2},{4,5},{5,4},{6,7},{7,6},{8,9},{9,8},{10,11... | collective-permute-start | bytes 393224 | tf_op jit(solution)/shard_map/ppermute | solution.py:279
  19.3 4.6 %collective-permute-start.6 = (f32[8,128]{1,0:T(8,128)S(1)}, f32[8,128]{1,0:T(8,128)S(1)}, u32[]{:S(2)}, u32[]{:S(2)}) collective-permute-start(f32[8,128]{1,0:T(8,128)S(1)} %add.10), channel_id=1, source_target_pairs={{0,8},{1,9},{2,10},{3,11},{4,12},{5,13},{6,14},{7,15},{8,0},{9,1},... | collective-permute-start | bytes 12296 | tf_op jit(solution)/shard_map/ppermute | solution.py:291
  23.8 1.2 %collective-permute-start.7 = (f32[8,128]{1,0:T(8,128)S(1)}, f32[8,128]{1,0:T(8,128)S(1)}, u32[]{:S(2)}, u32[]{:S(2)}) collective-permute-start(f32[8,128]{1,0:T(8,128)S(1)} %add.11.rest_0_), channel_id=1, source_target_pairs={{0,1},{1,0},{2,3},{3,2},{4,5},{5,4},{6,7},{7,6},{8,9},{9,8},{10,11... | collective-permute-start | bytes 12296 | tf_op jit(solution)/shard_map/ppermute | solution.py:291

commit v5 on v4

--- a/solution.py
+++ b/solution.py
@@ -250,10 +250,10 @@
 
 
 def final_kernel(
-    solution, residual, direction, image, from_across, from_within, *rest
+    solution, residual, direction, image, from_across, from_within, held,
+    solution_next, residual_next, step_length,
 ):
-    *held, solution_next, residual_next, step_length = rest
-    whole = tree_sum([part[...] for part in held])
+    whole = jnp.sum(held[...], axis=0)
     norm = jnp.concatenate([whole[:, 0:1], whole[:, 2:3]], axis=0)
     curvature = jnp.concatenate([whole[:, 1:2], whole[:, 3:4]], axis=0)
     step = norm / (curvature + EPSILON)
@@ -280,23 +280,19 @@
 
 
 def sum_steps(devices):
-    assert devices >= 4 and devices & (devices - 1) == 0
-    return [[1 << b] for b in range(1, devices.bit_length() - 1)] + [[1]]
-
-
-def partners(array, bits):
+    assert devices >= 8 and devices & (devices - 1) == 0
+    return [1 << b for b in range(1, devices.bit_length() - 2)] + [1 | devices // 2]
+
+
+def partner(array, bit):
+    return lax.ppermute(array, "orbit", [(i, i ^ bit) for i in range(lax.axis_size("orbit"))])
+
+
+def from_group(array, bits):
     devices = range(lax.axis_size("orbit"))
-    masks = [sum(bit for k, bit in enumerate(bits) if m >> k & 1) for m in range(1, 1 << len(bits))]
-    found = {
-        mask: lax.ppermute(array, "orbit", [(i, i ^ mask) for i in devices]) for mask in masks[::-1]
-    }
-    return [found[mask] for mask in masks]
-
-
-def tree_sum(parts):
-    while len(parts) > 1:
-        parts = [parts[k] + parts[k + 1] for k in range(0, len(parts), 2)]
-    return parts[0]
+    groups = [[i for i in devices if i & ~bits == low] for low in devices if low & bits == 0]
+    wide = jnp.broadcast_to(array[None], (len(groups[0]),) + array.shape)
+    return lax.all_to_all(wide, "orbit", 0, 0, axis_index_groups=groups)
 
 
 def local(
@@ -372,8 +368,8 @@
         crossing, live, rows, across, within, from_across, from_within, faced, norm, curved, jac,
         in_hbm(jacobian),
     )
-    near_step, *far_steps = sum_steps(devices)
-    held = [sums] + partners(sums, near_step)
+    *steps, last_bits = sum_steps(devices)
+    held = [sums, partner(sums, steps[0])]
 
     image, across, within = call(
         backward_kernel,
@@ -387,22 +383,21 @@
         ],
     )(crossing, length_class, live, smooth_weight, weighted, jac, late, begun, from_across, from_within)
     from_across = swapped_across(across)
-    within, *held = lax.optimization_barrier((within, *held))
-    sums = tree_sum(held)
-    held = [sums] + partners(sums, far_steps[0])
-    within, *held = lax.optimization_barrier((within, *held))
+    for step in steps[1:] + [None]:
+        within, *held = lax.optimization_barrier((within, *held))
+        sums = held[0] + held[1]
+        if step is not None:
+            held = [sums, partner(sums, step)]
     from_within = swapped_within(within)
-    for step in far_steps[1:]:
-        sums = tree_sum(held)
-        held = [sums] + partners(sums, step)
+    held = from_group(sums, last_bits)
 
     solution_next, residual_next, step_length = call(
         final_kernel,
         (whole, whole, shape((1, probes), f32)),
-        [VMEM()] * (6 + len(held)),
+        [VMEM()] * 7,
         8 * elements,
         28 * elements,
-    )(solution, residual, direction, image, from_across, from_within, *held)
+    )(solution, residual, direction, image, from_across, from_within, held)
     return solution_next, residual_next, step_length.reshape(probes)
 
 

time: 26.1 us -> 27.7 us (1.061)
  blocking collectives: 0 us -> 7.47 us
  waiting for transfers between devices: 7.07 us -> 0.81 us
  starting transfers between devices: 11 us -> 11.6 us
    all_to_all x0 -> x1, blocking collectives: none -> 7.47 us  [from_group(): return lax.all_to_all(wide, 'orbit', 0, 0, axis_index_groups=groups)]
    ppermute x4 -> x2, waiting for transfers between devices: 7.06 us -> 0.8 us  [partner(): lax.ppermute(array, 'orbit', [(i, i ^ bit) for i in range(lax.axis_size('...]
    ppermute x2, starting transfers between devices: 9.27 us -> 9.7 us  [swapped_across(): lax.ppermute(half, 'orbit', [(i, (i + 2 * (i % 2) - 1) % count) for i in...]
    ppermute x4 -> x2, starting transfers between devices: 1.76 us -> 1.88 us  [partner(): lax.ppermute(array, 'orbit', [(i, i ^ bit) for i in range(lax.axis_size('...]
  transfers between devices with their start and end apart: 8 -> 6, of which waited for: 3 -> 1; matrix products, arithmetic and copies ran while one was open for 0% -> 0% of each run, Pallas kernels for 12% -> 12%
where the time goes in v5:
time: 27.7 us; the launch traced here: 28 us
  starting transfers between devices  11.6 us (42%)
  blocking collectives  7.47 us (27%)
  Pallas kernels  6.71 us (24%)
  between operations  1.4 us (5%)
  waiting for transfers between devices  0.81 us (3%)
    ppermute x2, starting transfers between devices, swapped_across(): lax.ppermute(half, 'orbit', [(i, (i + 2 * (i % 2) - 1) % count) for i in...  9.7 us
    all_to_all x1, blocking collectives, from_group(): return lax.all_to_all(wide, 'orbit', 0, 0, axis_index_groups=groups)  7.47 us
    pallas_call x1, Pallas kernels, local(): call(inner_kernel, (shape((2 * cols,) + column, f32), shape((2, rim) + co...  2.16 us
    ppermute x2, starting transfers between devices, partner(): lax.ppermute(array, 'orbit', [(i, i ^ bit) for i in range(lax.axis_size('...  1.88 us
    pallas_call x1, Pallas kernels, local(): call(final_kernel, (whole, whole, shape((1, probes), f32)), [VMEM()] * 7,...  1.24 us
    pallas_call x1, Pallas kernels, local(): call(forward_kernel, (shape((slots, probes, width), bf16), shape((probes...  1.14 us
    pallas_call x1, Pallas kernels, local(): call(backward_kernel, (whole, near, near), [SMEM()] * 3 + [VMEM()] * 7, d...  1.1 us
    pallas_call x1, Pallas kernels, local(): call(rounding_kernel, (whole, near, near), [HBM()], 2 * elements, 10 * el...  1.07 us
  transfers between devices with their start and end apart: 6, of which 1 were waited for; matrix products, arithmetic and copies ran while one was open for 0% of the time, Pallas kernels for 12%

profile of v5, /device:TPU:0, one launch (start us, length us, event | category | flops | bytes accessed | tf_op | source)
XLA Modules:
  0.0 28.0 jit_solution(7186099264792188483)
XLA Ops:
  0.6 1.1 %shard_map.112 = (f32[8,8,16,128]{3,2,1,0:T(8,128)S(1)}, bf16[4,8,16,128]{3,2,1,0:T(8,128)(2,1)S(1)}, bf16[4,8,16,128]{3,2,1,0:T(8,128)(2,1)S(1)}) custom-call(f32[8,8,16,128]{3,2,1,0:T(8,128)} %direction.1), custom_call_target="tpu_custom_call" | custom-call | flops 262144 | bytes 1310720 | tf_op jit(solution)/shard_map/pallas_call | solution.py:316
  1.7 5.5 %collective-permute-start = (bf16[4,8,16,128]{3,2,1,0:T(8,128)(2,1)S(1)}, bf16[4,8,16,128]{3,2,1,0:T(8,128)(2,1)S(1)}, u32[]{:S(2)}, u32[]{:S(2)}) collective-permute-start(bf16[4,8,16,128]{3,2,1,0:T(8,128)(2,1)S(1)} %get-tuple-element.35.across), channel_id=1, source_target_pairs={{0,15},{1,2},{2,1},{3,4},{4,3},{5,6},{6,5},{7,8},{8,7},{9,10},{10,... | collective-permute-start | bytes 393224 | tf_op jit(solution)/shard_map/ppermute | solution.py:275
  7.2 0.0 collective-permute-start.1
  7.9 2.2 %shard_map.113 = (f32[16,8,16,128]{3,2,1,0:T(8,128)S(1)}, f32[2,4,8,16,128]{4,3,2,1,0:T(8,128)S(1)}, f32[16,128]{1,0:T(8,128)S(1)}, f32[16,128]{1,0:T(8,128)S(1)...) custom-call(f32[8,8,16,128]{3,2,1,0:T(8,128)S(1)} %get-tuple-element, ...), custom_call_target="tpu_custom_call" | custom-call | flops 7864320 | bytes 12582912 | tf_op jit(solution)/shard_map/pallas_call | solution.py:326
  10.0 0.0 collective-permute-done.from_across
  10.1 0.0 collective-permute-done.1.from_within
  10.1 0.0 copy-start.3
  10.1 1.1 %shard_map.114 = (bf16[8,16,128]{2,1,0:T(8,128)(2,1)S(1)}, f32[8,128]{1,0:T(8,128)S(1)}, bf16[2,24,128,128]{3,2,1,0:T(8,128)(2,1)S(1)}) custom-call(s32[8,24]{1,0:T(8,128)S(4)} %get-tuple-element.31.crossing, s32[8]{0:T(128)S(4)} %get-tuple-element.33.live, f32[8,128]{1,0:T(8,128)S(1)} %get-tuple-element.34.rows, ...), custom_call_target="tpu_custom_call" | custom-call | flops 100663296 | bytes 6291456 | tf_op jit(solution)/shard_map/pallas_call | solution.py:353
  11.2 0.0 copy-start
  11.2 0.0 copy-start.1
  11.2 0.0 copy-start.2
  11.3 1.8 %collective-permute-start.3 = (f32[8,128]{1,0:T(8,128)S(1)}, f32[8,128]{1,0:T(8,128)S(1)}, u32[]{:S(2)}, u32[]{:S(2)}) collective-permute-start(f32[8,128]{1,0:T(8,128)S(1)} %get-tuple-element.49), channel_id=1, source_target_pairs={{0,2},{1,3},{2,0},{3,1},{4,6},{5,7},{6,4},{7,5},{8,10},{9,11},{10,... | collective-permute-start | bytes 12296 | tf_op jit(solution)/shard_map/ppermute | solution.py:288
  13.0 0.0 copy-done.3
  13.0 1.1 %shard_map.115 = (f32[8,8,16,128]{3,2,1,0:T(8,128)S(1)}, bf16[4,8,16,128]{3,2,1,0:T(8,128)(2,1)S(1)}, bf16[4,8,16,128]{3,2,1,0:T(8,128)(2,1)S(1)}) custom-call(s32[8,24]{1,0:T(8,128)S(4)} %get-tuple-element.31.crossing, s32[128]{0:T(128)S(4)} %get-tuple-element.32.classes, s32[8]{0:T(128)S(4)} %get-tuple-element.33.live, f32[8,128]{1,0:T(8,128)S(1)} %copy-done.3, ...), custom_call_target="tpu_custom_call" | custom-call | flops 100663296 | bytes 6291456 | tf_op jit(solution)/shard_map/pallas_call | solution.py:374
  14.1 0.8 %collective-permute-done.3 = f32[8,128]{1,0:T(8,128)S(1)} collective-permute-done((f32[8,128]{1,0:T(8,128)S(1)}, f32[8,128]{1,0:T(8,128)S(1)}, u32[]{:S(2)}, u32[]{:S(2)}) %collective-permute-start.3) | collective-permute-done | bytes 4128 | tf_op jit(solution)/shard_map/ppermute | solution.py:288
  14.9 0.1 collective-permute-start.4
  15.1 4.2 %collective-permute-start.2 = (bf16[4,8,16,128]{3,2,1,0:T(8,128)(2,1)S(1)}, bf16[4,8,16,128]{3,2,1,0:T(8,128)(2,1)S(1)}, u32[]{:S(2)}, u32[]{:S(2)}) collective-permute-start(bf16[4,8,16,128]{3,2,1,0:T(8,128)(2,1)S(1)} %get-tuple-element.45), channel_id=1, source_target_pairs={{0,15},{1,2},{2,1},{3,4},{4,3},{5,6},{6,5},{7,8},{8,7},{9,10},{10,... | collective-permute-start | bytes 393224 | tf_op jit(solution)/shard_map/ppermute | solution.py:275
  19.2 0.0 collective-permute-done.4
  19.3 0.0 collective-permute-start.5
  19.3 7.5 %all_to_all.5.held = f32[4,8,128]{2,1,0:T(8,128)S(1)} all-to-all(f32[4,8,128]{2,1,0:T(8,128)S(1)} %broadcast_in_dim.2), channel_id=1, replica_groups={{0,1,8,9},{2,3,10,11},{4,5,12,13},{6,7,14,15},{16,17,24,25},{18,19,26,2..., dimensions={0} | all-to-all | bytes 32768 | tf_op jit(solution)/shard_map/all_to_all | solution.py:295
  26.7 0.0 collective-permute-done.2.from_across
  26.7 0.0 collective-permute-done.5.from_within
  26.7 0.0 copy-done
  26.8 0.0 copy-done.1
  26.8 0.0 copy-done.2
  26.8 1.2 %shard_map.116 = (f32[8,8,16,128]{3,2,1,0:T(8,128)}, f32[8,8,16,128]{3,2,1,0:T(8,128)}, f32[1,16]{1,0:T(1,128)}) custom-call(f32[8,8,16,128]{3,2,1,0:T(8,128)S(1)} %copy-done.2, f32[8,8,16,128]{3,2,1,0:T(8,128)S(1)} %copy-done.1, f32[8,8,16,128]{3,2,1,0:T(8,128)S(1)} %copy-done, f32[8,8,16,128]{3,2,1,0:T(8,128)S(1)} %get-tuple-element.44.image, ...), custom_call_target="tpu_custom_call" | custom-call | flops 1048576 | bytes 3670016 | tf_op jit(solution)/shard_map/pallas_call | solution.py:394
  (3 shorter events, 0.0 us)
Async XLA Ops:
  1.7 8.3 %collective-permute-start = (bf16[4,8,16,128]{3,2,1,0:T(8,128)(2,1)S(1)}, bf16[4,8,16,128]{3,2,1,0:T(8,128)(2,1)S(1)}, u32[]{:S(2)}, u32[]{:S(2)}) collective-permute-start(bf16[4,8,16,128]{3,2,1,0:T(8,128)(2,1)S(1)} %get-tuple-element.35.across), channel_id=1, source_target_pairs={{0,15},{1,2},{2,1},{3,4},{4,3},{5,6},{6,5},{7,8},{8,7},{9,10},{10,... | collective-permute-start | bytes 393224 | tf_op jit(solution)/shard_map/ppermute | solution.py:275
  7.2 2.8 %collective-permute-start.1 = (bf16[4,8,16,128]{3,2,1,0:T(8,128)(2,1)S(1)}, bf16[4,8,16,128]{3,2,1,0:T(8,128)(2,1)S(1)}, u32[]{:S(2)}, u32[]{:S(2)}) collective-permute-start(bf16[4,8,16,128]{3,2,1,0:T(8,128)(2,1)S(1)} %get-tuple-element.36.within), channel_id=1, source_target_pairs={{0,1},{1,0},{2,3},{3,2},{4,5},{5,4},{6,7},{7,6},{8,9},{9,8},{10,11... | collective-permute-start | bytes 393224 | tf_op jit(solution)/shard_map/ppermute | solution.py:279
  10.1 3.0 %copy-start.3 = (f32[8,128]{1,0:T(8,128)S(1)}, f32[8,128]{1,0:T(8,128)}, u32[]{:S(2)}) copy-start(f32[8,128]{1,0:T(8,128)} %smooth.1) | copy-start | bytes 12292
  11.2 15.5 %copy-start = (f32[8,8,16,128]{3,2,1,0:T(8,128)S(1)}, f32[8,8,16,128]{3,2,1,0:T(8,128)}, u32[]{:S(2)}) copy-start(f32[8,8,16,128]{3,2,1,0:T(8,128)} %direction.1) | copy-start | bytes 1572868
  11.2 15.5 %copy-start.1 = (f32[8,8,16,128]{3,2,1,0:T(8,128)S(1)}, f32[8,8,16,128]{3,2,1,0:T(8,128)}, u32[]{:S(2)}) copy-start(f32[8,8,16,128]{3,2,1,0:T(8,128)} %residual.1) | copy-start | bytes 1572868
  11.2 15.5 %copy-start.2 = (f32[8,8,16,128]{3,2,1,0:T(8,128)S(1)}, f32[8,8,16,128]{3,2,1,0:T(8,128)}, u32[]{:S(2)}) copy-start(f32[8,8,16,128]{3,2,1,0:T(8,128)} %solution.1) | copy-start | bytes 1572868
  11.3 3.7 %collective-permute-start.3 = (f32[8,128]{1,0:T(8,128)S(1)}, f32[8,128]{1,0:T(8,128)S(1)}, u32[]{:S(2)}, u32[]{:S(2)}) collective-permute-start(f32[8,128]{1,0:T(8,128)S(1)} %get-tuple-element.49), channel_id=1, source_target_pairs={{0,2},{1,3},{2,0},{3,1},{4,6},{5,7},{6,4},{7,5},{8,10},{9,11},{10,... | collective-permute-start | bytes 12296 | tf_op jit(solution)/shard_map/ppermute | solution.py:288
  14.9 4.3 %collective-permute-start.4 = (f32[8,128]{1,0:T(8,128)S(1)}, f32[8,128]{1,0:T(8,128)S(1)}, u32[]{:S(2)}, u32[]{:S(2)}) collective-permute-start(f32[8,128]{1,0:T(8,128)S(1)} %add.6), channel_id=1, source_target_pairs={{0,4},{1,5},{2,6},{3,7},{4,0},{5,1},{6,2},{7,3},{8,12},{9,13},{10,... | collective-permute-start | bytes 12296 | tf_op jit(solution)/shard_map/ppermute | solution.py:288
  15.1 11.7 %collective-permute-start.2 = (bf16[4,8,16,128]{3,2,1,0:T(8,128)(2,1)S(1)}, bf16[4,8,16,128]{3,2,1,0:T(8,128)(2,1)S(1)}, u32[]{:S(2)}, u32[]{:S(2)}) collective-permute-start(bf16[4,8,16,128]{3,2,1,0:T(8,128)(2,1)S(1)} %get-tuple-element.45), channel_id=1, source_target_pairs={{0,15},{1,2},{2,1},{3,4},{4,3},{5,6},{6,5},{7,8},{8,7},{9,10},{10,... | collective-permute-start | bytes 393224 | tf_op jit(solution)/shard_map/ppermute | solution.py:275
  19.3 7.5 %collective-permute-start.5 = (bf16[4,8,16,128]{3,2,1,0:T(8,128)(2,1)S(1)}, bf16[4,8,16,128]{3,2,1,0:T(8,128)(2,1)S(1)}, u32[]{:S(2)}, u32[]{:S(2)}) collective-permute-start(bf16[4,8,16,128]{3,2,1,0:T(8,128)(2,1)S(1)} %get-tuple-element.51), channel_id=1, source_target_pairs={{0,1},{1,0},{2,3},{3,2},{4,5},{5,4},{6,7},{7,6},{8,9},{9,8},{10,11... | collective-permute-start | bytes 393224 | tf_op jit(solution)/shard_map/ppermute | solution.py:279

commit v6 on v0

--- a/solution.py
+++ b/solution.py
@@ -266,7 +266,7 @@
 
 def sum_steps(devices):
     assert devices >= 8 and devices & (devices - 1) == 0
-    return [[1 << b] for b in range(1, devices.bit_length() - 2)] + [[1, devices // 2]]
+    return [[2]] + [[1 << b] for b in range(devices.bit_length() - 2, 2, -1)] + [[1, 4]]
 
 
 def partners(array, bits):

time: 26.5 us -> 25.3 us (0.955); the launches traced: 26.8 us -> 25.1 us
  Pallas kernels: 9.39 us -> 5.39 us
  starting transfers between devices: 10.4 us -> 11.6 us
  waiting for transfers between devices: 5.55 us -> 6.71 us
    ppermute x5, starting transfers between devices: 2.77 us -> 4.63 us  [partners(): lax.ppermute(array, 'orbit', [(i, i ^ mask) for i in devices])]
    pallas_call x1, Pallas kernels: 2.18 us -> 0.63 us  [local(): call(forward_kernel, (shape((slots, probes, width), bf16), shape((probes...]
    pallas_call x1, Pallas kernels: 3.11 us -> 1.7 us  [local(): call(inner_kernel, (shape((2 * cols,) + column, f32), shape((2, rim) + co...]
    pallas_call x1, Pallas kernels: 1.79 us -> 0.75 us  [local(): call(backward_kernel, (whole, near, near), [SMEM()] * 3 + [VMEM()] * 6, d...]
    ppermute x5, waiting for transfers between devices: 5.54 us -> 6.42 us  [partners(): lax.ppermute(array, 'orbit', [(i, i ^ mask) for i in devices])]
    ppermute x2, starting transfers between devices: 7.63 us -> 6.96 us  [swapped_across(): lax.ppermute(half, 'orbit', [(i, (i + 2 * (i % 2) - 1) % count) for i in...]
    ppermute x2, waiting for transfers between devices: 0.01 us -> 0.28 us  [swapped_across(): lax.ppermute(half, 'orbit', [(i, (i + 2 * (i % 2) - 1) % count) for i in...]
  transfers between devices with their start and end apart: 9 -> 9, of which waited for: 3 -> 5; matrix products, arithmetic and copies ran while one was open for 0% -> 0% of each run, Pallas kernels for 18% -> 10%
where the time goes in v6:
time: 25.3 us; the launch traced here: 25.1 us
  starting transfers between devices  11.6 us (46%)
  waiting for transfers between devices  6.71 us (27%)
  Pallas kernels  5.39 us (21%)
  between operations  1.35 us (5%)
    ppermute x2, starting transfers between devices, swapped_across(): lax.ppermute(half, 'orbit', [(i, (i + 2 * (i % 2) - 1) % count) for i in...  6.96 us
    ppermute x5, waiting for transfers between devices, partners(): lax.ppermute(array, 'orbit', [(i, i ^ mask) for i in devices])  6.42 us
    ppermute x5, starting transfers between devices, partners(): lax.ppermute(array, 'orbit', [(i, i ^ mask) for i in devices])  4.63 us
    pallas_call x1, Pallas kernels, local(): call(inner_kernel, (shape((2 * cols,) + column, f32), shape((2, rim) + co...  1.7 us
    pallas_call x1, Pallas kernels, local(): call(final_kernel, (whole, whole, shape((1, probes), f32)), [VMEM()] * (6...  1.24 us
    pallas_call x1, Pallas kernels, local(): call(rounding_kernel, (whole, near, near), [HBM()], 2 * elements, 10 * el...  1.07 us
    pallas_call x1, Pallas kernels, local(): call(backward_kernel, (whole, near, near), [SMEM()] * 3 + [VMEM()] * 6, d...  0.75 us
    pallas_call x1, Pallas kernels, local(): call(forward_kernel, (shape((slots, probes, width), bf16), shape((probes...  0.63 us
  transfers between devices with their start and end apart: 9, of which 5 were waited for; matrix products, arithmetic and copies ran while one was open for 0% of the time, Pallas kernels for 10%

profile of v6, /device:TPU:0, one launch (start us, length us, event | category | flops | bytes accessed | tf_op | source)
XLA Modules:
  0.0 25.1 jit_solution(3040366877221700662)
XLA Ops:
  0.6 1.1 %shard_map.112 = (f32[8,8,16,128]{3,2,1,0:T(8,128)S(1)}, bf16[4,8,16,128]{3,2,1,0:T(8,128)(2,1)S(1)}, bf16[4,8,16,128]{3,2,1,0:T(8,128)(2,1)S(1)}) custom-call(f32[8,8,16,128]{3,2,1,0:T(8,128)} %direction.1), custom_call_target="tpu_custom_call" | custom-call | flops 262144 | bytes 1310720 | tf_op jit(solution)/shard_map/pallas_call | solution.py:304
  1.7 5.5 %collective-permute-start = (bf16[4,8,16,128]{3,2,1,0:T(8,128)(2,1)S(1)}, bf16[4,8,16,128]{3,2,1,0:T(8,128)(2,1)S(1)}, u32[]{:S(2)}, u32[]{:S(2)}) collective-permute-start(bf16[4,8,16,128]{3,2,1,0:T(8,128)(2,1)S(1)} %get-tuple-element.34.across), channel_id=1, source_target_pairs={{0,15},{1,2},{2,1},{3,4},{4,3},{5,6},{6,5},{7,8},{8,7},{9,10},{10,... | collective-permute-start | bytes 393224 | tf_op jit(solution)/shard_map/ppermute | solution.py:260
  7.2 0.0 collective-permute-start.1
  7.9 0.0 copy-start.3
  7.9 1.7 %shard_map.113 = (f32[16,8,16,128]{3,2,1,0:T(8,128)S(1)}, f32[2,4,8,16,128]{4,3,2,1,0:T(8,128)S(1)}, f32[16,128]{1,0:T(8,128)S(1)}, f32[16,128]{1,0:T(8,128)S(1)...) custom-call(f32[8,8,16,128]{3,2,1,0:T(8,128)S(1)} %get-tuple-element, ...), custom_call_target="tpu_custom_call" | custom-call | flops 7864320 | bytes 12582912 | tf_op jit(solution)/shard_map/pallas_call | solution.py:314
  9.6 0.3 %collective-permute-done.from_across = bf16[4,8,16,128]{3,2,1,0:T(8,128)(2,1)S(1)} collective-permute-done((bf16[4,8,16,128]{3,2,1,0:T(8,128)(2,1)S(1)}, bf16[4,8,16,128]{3,2,1,0:T(8,128)(2,1)S(1)}, u32[]{:S(2)}, u32[]{:S(2)}) %collective-permute-start) | collective-permute-done | bytes 131104 | tf_op jit(solution)/shard_map/ppermute | solution.py:260
  9.9 0.0 collective-permute-done.1.from_within
  9.9 0.0 copy-start
  9.9 0.0 copy-start.1
  9.9 0.0 copy-start.2
  9.9 0.6 %shard_map.114 = (bf16[8,16,128]{2,1,0:T(8,128)(2,1)S(1)}, f32[8,128]{1,0:T(8,128)S(1)}) custom-call(s32[8,24]{1,0:T(8,128)S(4)} %get-tuple-element.30.crossing, s32[8]{0:T(128)S(4)} %get-tuple-element.32.live, f32[8,128]{1,0:T(8,128)S(1)} %get-tuple-element.33.rows, bf16[4,8,16,128]{3,2,1,0:T(8,128)(2,1)S(1)} %get-tuple-element.34.across, ...), custom_call_target="tpu_custom_call" | custom-call | flops 100663296 | bytes 6291456 | tf_op jit(solution)/shard_map/pallas_call | solution.py:341
  10.5 0.7 %collective-permute-start.3 = (f32[8,128]{1,0:T(8,128)S(1)}, f32[8,128]{1,0:T(8,128)S(1)}, u32[]{:S(2)}, u32[]{:S(2)}) collective-permute-start(f32[8,128]{1,0:T(8,128)S(1)} %get-tuple-element.47), channel_id=1, source_target_pairs={{0,2},{1,3},{2,0},{3,1},{4,6},{5,7},{6,4},{7,5},{8,10},{9,11},{10,... | collective-permute-start | bytes 12296 | tf_op jit(solution)/shard_map/ppermute | solution.py:276
  11.2 0.0 copy-done.3
  11.2 0.8 %shard_map.115 = (f32[8,8,16,128]{3,2,1,0:T(8,128)S(1)}, bf16[4,8,16,128]{3,2,1,0:T(8,128)(2,1)S(1)}, bf16[4,8,16,128]{3,2,1,0:T(8,128)(2,1)S(1)}) custom-call(s32[8,24]{1,0:T(8,128)S(4)} %get-tuple-element.30.crossing, s32[128]{0:T(128)S(4)} %get-tuple-element.31.classes, s32[8]{0:T(128)S(4)} %get-tuple-element.32.live, f32[8,128]{1,0:T(8,128)S(1)} %copy-done.3, ...), custom_call_target="tpu_custom_call" | custom-call | flops 100663296 | bytes 6291456 | tf_op jit(solution)/shard_map/pallas_call | solution.py:352
  12.0 2.2 %collective-permute-done.3 = f32[8,128]{1,0:T(8,128)S(1)} collective-permute-done((f32[8,128]{1,0:T(8,128)S(1)}, f32[8,128]{1,0:T(8,128)S(1)}, u32[]{:S(2)}, u32[]{:S(2)}) %collective-permute-start.3) | collective-permute-done | bytes 4128 | tf_op jit(solution)/shard_map/ppermute | solution.py:276
  14.1 1.8 %collective-permute-start.4 = (f32[8,128]{1,0:T(8,128)S(1)}, f32[8,128]{1,0:T(8,128)S(1)}, u32[]{:S(2)}, u32[]{:S(2)}) collective-permute-start(f32[8,128]{1,0:T(8,128)S(1)} %add.6), channel_id=1, source_target_pairs={{0,8},{1,9},{2,10},{3,11},{4,12},{5,13},{6,14},{7,15},{8,0},{9,1},... | collective-permute-start | bytes 12296 | tf_op jit(solution)/shard_map/ppermute | solution.py:276
  16.0 1.4 %collective-permute-start.2 = (bf16[4,8,16,128]{3,2,1,0:T(8,128)(2,1)S(1)}, bf16[4,8,16,128]{3,2,1,0:T(8,128)(2,1)S(1)}, u32[]{:S(2)}, u32[]{:S(2)}) collective-permute-start(bf16[4,8,16,128]{3,2,1,0:T(8,128)(2,1)S(1)} %get-tuple-element.43), channel_id=1, source_target_pairs={{0,15},{1,2},{2,1},{3,4},{4,3},{5,6},{6,5},{7,8},{8,7},{9,10},{10,... | collective-permute-start | bytes 393224 | tf_op jit(solution)/shard_map/ppermute | solution.py:260
  17.4 1.2 %collective-permute-done.4 = f32[8,128]{1,0:T(8,128)S(1)} collective-permute-done((f32[8,128]{1,0:T(8,128)S(1)}, f32[8,128]{1,0:T(8,128)S(1)}, u32[]{:S(2)}, u32[]{:S(2)}) %collective-permute-start.4) | collective-permute-done | bytes 4128 | tf_op jit(solution)/shard_map/ppermute | solution.py:276
  18.6 0.0 collective-permute-start.5
  18.6 0.5 %collective-permute-start.6 = (f32[8,128]{1,0:T(8,128)S(1)}, f32[8,128]{1,0:T(8,128)S(1)}, u32[]{:S(2)}, u32[]{:S(2)}) collective-permute-start(f32[8,128]{1,0:T(8,128)S(1)} %add.7.rest_0_), channel_id=1, source_target_pairs={{0,1},{1,0},{2,3},{3,2},{4,5},{5,4},{6,7},{7,6},{8,9},{9,8},{10,11... | collective-permute-start | bytes 12296 | tf_op jit(solution)/shard_map/ppermute | solution.py:276
  19.2 1.6 %collective-permute-start.7 = (f32[8,128]{1,0:T(8,128)S(1)}, f32[8,128]{1,0:T(8,128)S(1)}, u32[]{:S(2)}, u32[]{:S(2)}) collective-permute-start(f32[8,128]{1,0:T(8,128)S(1)} %add.7.rest_0_), channel_id=1, source_target_pairs={{0,4},{1,5},{2,6},{3,7},{4,0},{5,1},{6,2},{7,3},{8,12},{9,13},{10,... | collective-permute-start | bytes 12296 | tf_op jit(solution)/shard_map/ppermute | solution.py:276
  20.8 0.0 collective-permute-start.8
  20.8 0.0 collective-permute-done.6.rest_1_
  20.8 2.0 %collective-permute-done.7.rest_2_ = f32[8,128]{1,0:T(8,128)S(1)} collective-permute-done((f32[8,128]{1,0:T(8,128)S(1)}, f32[8,128]{1,0:T(8,128)S(1)}, u32[]{:S(2)}, u32[]{:S(2)}) %collective-permute-start.7) | collective-permute-done | bytes 4128 | tf_op jit(solution)/shard_map/ppermute | solution.py:276
  22.8 1.0 %collective-permute-done.8.rest_3_ = f32[8,128]{1,0:T(8,128)S(1)} collective-permute-done((f32[8,128]{1,0:T(8,128)S(1)}, f32[8,128]{1,0:T(8,128)S(1)}, u32[]{:S(2)}, u32[]{:S(2)}) %collective-permute-start.8) | collective-permute-done | bytes 4128 | tf_op jit(solution)/shard_map/ppermute | solution.py:276
  23.8 0.0 collective-permute-done.2.from_across
  23.8 0.0 collective-permute-done.5.from_within
  23.8 0.0 copy-done
  23.8 0.0 copy-done.1
  23.8 0.0 copy-done.2
  23.8 1.2 %shard_map.116 = (f32[8,8,16,128]{3,2,1,0:T(8,128)}, f32[8,8,16,128]{3,2,1,0:T(8,128)}, f32[1,16]{1,0:T(1,128)}) custom-call(f32[8,8,16,128]{3,2,1,0:T(8,128)S(1)} %copy-done.2, f32[8,8,16,128]{3,2,1,0:T(8,128)S(1)} %copy-done.1, f32[8,8,16,128]{3,2,1,0:T(8,128)S(1)} %copy-done, f32[8,8,16,128]{3,2,1,0:T(8,128)S(1)} %get-tuple-element.42.image, ...), custom_call_target="tpu_custom_call" | custom-call | flops 1048576 | bytes 3670016 | tf_op jit(solution)/shard_map/pallas_call | solution.py:373
  (2 shorter events, 0.0 us)
Async XLA Ops:
  1.7 8.2 %collective-permute-start = (bf16[4,8,16,128]{3,2,1,0:T(8,128)(2,1)S(1)}, bf16[4,8,16,128]{3,2,1,0:T(8,128)(2,1)S(1)}, u32[]{:S(2)}, u32[]{:S(2)}) collective-permute-start(bf16[4,8,16,128]{3,2,1,0:T(8,128)(2,1)S(1)} %get-tuple-element.34.across), channel_id=1, source_target_pairs={{0,15},{1,2},{2,1},{3,4},{4,3},{5,6},{6,5},{7,8},{8,7},{9,10},{10,... | collective-permute-start | bytes 393224 | tf_op jit(solution)/shard_map/ppermute | solution.py:260
  7.2 2.7 %collective-permute-start.1 = (bf16[4,8,16,128]{3,2,1,0:T(8,128)(2,1)S(1)}, bf16[4,8,16,128]{3,2,1,0:T(8,128)(2,1)S(1)}, u32[]{:S(2)}, u32[]{:S(2)}) collective-permute-start(bf16[4,8,16,128]{3,2,1,0:T(8,128)(2,1)S(1)} %get-tuple-element.35.within), channel_id=1, source_target_pairs={{0,1},{1,0},{2,3},{3,2},{4,5},{5,4},{6,7},{7,6},{8,9},{9,8},{10,11... | collective-permute-start | bytes 393224 | tf_op jit(solution)/shard_map/ppermute | solution.py:264
  7.9 3.3 %copy-start.3 = (f32[8,128]{1,0:T(8,128)S(1)}, f32[8,128]{1,0:T(8,128)}, u32[]{:S(2)}) copy-start(f32[8,128]{1,0:T(8,128)} %smooth.1) | copy-start | bytes 12292
  9.9 13.9 %copy-start = (f32[8,8,16,128]{3,2,1,0:T(8,128)S(1)}, f32[8,8,16,128]{3,2,1,0:T(8,128)}, u32[]{:S(2)}) copy-start(f32[8,8,16,128]{3,2,1,0:T(8,128)} %direction.1) | copy-start | bytes 1572868
  9.9 13.9 %copy-start.1 = (f32[8,8,16,128]{3,2,1,0:T(8,128)S(1)}, f32[8,8,16,128]{3,2,1,0:T(8,128)}, u32[]{:S(2)}) copy-start(f32[8,8,16,128]{3,2,1,0:T(8,128)} %residual.1) | copy-start | bytes 1572868
  9.9 13.9 %copy-start.2 = (f32[8,8,16,128]{3,2,1,0:T(8,128)S(1)}, f32[8,8,16,128]{3,2,1,0:T(8,128)}, u32[]{:S(2)}) copy-start(f32[8,8,16,128]{3,2,1,0:T(8,128)} %solution.1) | copy-start | bytes 1572868
  10.5 3.6 %collective-permute-start.3 = (f32[8,128]{1,0:T(8,128)S(1)}, f32[8,128]{1,0:T(8,128)S(1)}, u32[]{:S(2)}, u32[]{:S(2)}) collective-permute-start(f32[8,128]{1,0:T(8,128)S(1)} %get-tuple-element.47), channel_id=1, source_target_pairs={{0,2},{1,3},{2,0},{3,1},{4,6},{5,7},{6,4},{7,5},{8,10},{9,11},{10,... | collective-permute-start | bytes 12296 | tf_op jit(solution)/shard_map/ppermute | solution.py:276
  14.1 4.5 %collective-permute-start.4 = (f32[8,128]{1,0:T(8,128)S(1)}, f32[8,128]{1,0:T(8,128)S(1)}, u32[]{:S(2)}, u32[]{:S(2)}) collective-permute-start(f32[8,128]{1,0:T(8,128)S(1)} %add.6), channel_id=1, source_target_pairs={{0,8},{1,9},{2,10},{3,11},{4,12},{5,13},{6,14},{7,15},{8,0},{9,1},... | collective-permute-start | bytes 12296 | tf_op jit(solution)/shard_map/ppermute | solution.py:276
  16.0 7.8 %collective-permute-start.2 = (bf16[4,8,16,128]{3,2,1,0:T(8,128)(2,1)S(1)}, bf16[4,8,16,128]{3,2,1,0:T(8,128)(2,1)S(1)}, u32[]{:S(2)}, u32[]{:S(2)}) collective-permute-start(bf16[4,8,16,128]{3,2,1,0:T(8,128)(2,1)S(1)} %get-tuple-element.43), channel_id=1, source_target_pairs={{0,15},{1,2},{2,1},{3,4},{4,3},{5,6},{6,5},{7,8},{8,7},{9,10},{10,... | collective-permute-start | bytes 393224 | tf_op jit(solution)/shard_map/ppermute | solution.py:260
  18.6 5.2 %collective-permute-start.5 = (bf16[4,8,16,128]{3,2,1,0:T(8,128)(2,1)S(1)}, bf16[4,8,16,128]{3,2,1,0:T(8,128)(2,1)S(1)}, u32[]{:S(2)}, u32[]{:S(2)}) collective-permute-start(bf16[4,8,16,128]{3,2,1,0:T(8,128)(2,1)S(1)} %get-tuple-element.49), channel_id=1, source_target_pairs={{0,1},{1,0},{2,3},{3,2},{4,5},{5,4},{6,7},{7,6},{8,9},{9,8},{10,11... | collective-permute-start | bytes 393224 | tf_op jit(solution)/shard_map/ppermute | solution.py:264
  18.6 2.1 %collective-permute-start.6 = (f32[8,128]{1,0:T(8,128)S(1)}, f32[8,128]{1,0:T(8,128)S(1)}, u32[]{:S(2)}, u32[]{:S(2)}) collective-permute-start(f32[8,128]{1,0:T(8,128)S(1)} %add.7.rest_0_), channel_id=1, source_target_pairs={{0,1},{1,0},{2,3},{3,2},{4,5},{5,4},{6,7},{7,6},{8,9},{9,8},{10,11... | collective-permute-start | bytes 12296 | tf_op jit(solution)/shard_map/ppermute | solution.py:276
  19.2 3.6 %collective-permute-start.7 = (f32[8,128]{1,0:T(8,128)S(1)}, f32[8,128]{1,0:T(8,128)S(1)}, u32[]{:S(2)}, u32[]{:S(2)}) collective-permute-start(f32[8,128]{1,0:T(8,128)S(1)} %add.7.rest_0_), channel_id=1, source_target_pairs={{0,4},{1,5},{2,6},{3,7},{4,0},{5,1},{6,2},{7,3},{8,12},{9,13},{10,... | collective-permute-start | bytes 12296 | tf_op jit(solution)/shard_map/ppermute | solution.py:276
  20.8 3.0 %collective-permute-start.8 = (f32[8,128]{1,0:T(8,128)S(1)}, f32[8,128]{1,0:T(8,128)S(1)}, u32[]{:S(2)}, u32[]{:S(2)}) collective-permute-start(f32[8,128]{1,0:T(8,128)S(1)} %add.7.rest_0_), channel_id=1, source_target_pairs={{0,5},{1,4},{2,7},{3,6},{4,1},{5,0},{6,3},{7,2},{8,13},{9,12},{10,... | collective-permute-start | bytes 12296 | tf_op jit(solution)/shard_map/ppermute | solution.py:276

commit v7 on v6

--- a/solution.py
+++ b/solution.py
@@ -85,7 +85,8 @@
 
 
 def slot_groups(slots):
-    return [range(i, min(i + GROUP, slots)) for i in range(0, slots, GROUP)]
+    ends = [end for end in (GROUP, 2 * GROUP) if end < slots] + [slots]
+    return [range(begin, end) for begin, end in zip([0] + ends, ends)]
 
 
 def if_live(count, group, work):

time: 25.3 us -> 25.5 us (level)
  starting transfers between devices: 11.6 us -> 14 us
  waiting for transfers between devices: 6.71 us -> 4.6 us
    ppermute x5, waiting for transfers between devices: 6.42 us -> 3.38 us  [partners(): lax.ppermute(array, 'orbit', [(i, i ^ mask) for i in devices])]
    ppermute x5, starting transfers between devices: 4.63 us -> 6.74 us  [partners(): lax.ppermute(array, 'orbit', [(i, i ^ mask) for i in devices])]
    ppermute x2, waiting for transfers between devices: 0.28 us -> 1.22 us  [swapped_across(): lax.ppermute(half, 'orbit', [(i, (i + 2 * (i % 2) - 1) % count) for i in...]
    ppermute x2, starting transfers between devices: 0.01 us -> 0.86 us  [swapped_within(): lax.ppermute(half, 'orbit', [(i, i ^ 1) for i in range(lax.axis_size('orb...]
    ppermute x2, starting transfers between devices: 6.96 us -> 6.45 us  [swapped_across(): lax.ppermute(half, 'orbit', [(i, (i + 2 * (i % 2) - 1) % count) for i in...]
where the time goes in v7:
time: 25.5 us; the launch traced here: 25.4 us
  starting transfers between devices  14 us (55%)
  Pallas kernels  5.37 us (21%)
  waiting for transfers between devices  4.6 us (18%)
  between operations  1.34 us (5%)
    ppermute x5, starting transfers between devices, partners(): lax.ppermute(array, 'orbit', [(i, i ^ mask) for i in devices])  6.74 us
    ppermute x2, starting transfers between devices, swapped_across(): lax.ppermute(half, 'orbit', [(i, (i + 2 * (i % 2) - 1) % count) for i in...  6.45 us
    ppermute x5, waiting for transfers between devices, partners(): lax.ppermute(array, 'orbit', [(i, i ^ mask) for i in devices])  3.38 us
    pallas_call x1, Pallas kernels, local(): call(inner_kernel, (shape((2 * cols,) + column, f32), shape((2, rim) + co...  1.68 us
    pallas_call x1, Pallas kernels, local(): call(final_kernel, (whole, whole, shape((1, probes), f32)), [VMEM()] * (6...  1.24 us
    ppermute x2, waiting for transfers between devices, swapped_across(): lax.ppermute(half, 'orbit', [(i, (i + 2 * (i % 2) - 1) % count) for i in...  1.22 us
    pallas_call x1, Pallas kernels, local(): call(rounding_kernel, (whole, near, near), [HBM()], 2 * elements, 10 * el...  1.07 us
    ppermute x2, starting transfers between devices, swapped_within(): lax.ppermute(half, 'orbit', [(i, i ^ 1) for i in range(lax.axis_size('orb...  0.86 us
  transfers between devices with their start and end apart: 9, of which 5 were waited for; matrix products, arithmetic and copies ran while one was open for 0% of the time, Pallas kernels for 10%

profile of v7, /device:TPU:0, one launch (start us, length us, event | category | flops | bytes accessed | tf_op | source)
XLA Modules:
  0.0 25.4 jit_solution(7056263670072015591)
XLA Ops:
  0.6 1.1 %shard_map.112 = (f32[8,8,16,128]{3,2,1,0:T(8,128)S(1)}, bf16[4,8,16,128]{3,2,1,0:T(8,128)(2,1)S(1)}, bf16[4,8,16,128]{3,2,1,0:T(8,128)(2,1)S(1)}) custom-call(f32[8,8,16,128]{3,2,1,0:T(8,128)} %direction.1), custom_call_target="tpu_custom_call" | custom-call | flops 262144 | bytes 1310720 | tf_op jit(solution)/shard_map/pallas_call | solution.py:305
  1.7 5.5 %collective-permute-start = (bf16[4,8,16,128]{3,2,1,0:T(8,128)(2,1)S(1)}, bf16[4,8,16,128]{3,2,1,0:T(8,128)(2,1)S(1)}, u32[]{:S(2)}, u32[]{:S(2)}) collective-permute-start(bf16[4,8,16,128]{3,2,1,0:T(8,128)(2,1)S(1)} %get-tuple-element.34.across), channel_id=1, source_target_pairs={{0,15},{1,2},{2,1},{3,4},{4,3},{5,6},{6,5},{7,8},{8,7},{9,10},{10,... | collective-permute-start | bytes 393224 | tf_op jit(solution)/shard_map/ppermute | solution.py:261
  7.2 0.0 collective-permute-start.1
  7.9 0.0 copy-start.3
  7.9 1.7 %shard_map.113 = (f32[16,8,16,128]{3,2,1,0:T(8,128)S(1)}, f32[2,4,8,16,128]{4,3,2,1,0:T(8,128)S(1)}, f32[16,128]{1,0:T(8,128)S(1)}, f32[16,128]{1,0:T(8,128)S(1)...) custom-call(f32[8,8,16,128]{3,2,1,0:T(8,128)S(1)} %get-tuple-element, ...), custom_call_target="tpu_custom_call" | custom-call | flops 7864320 | bytes 12582912 | tf_op jit(solution)/shard_map/pallas_call | solution.py:315
  9.6 0.3 %collective-permute-done.from_across = bf16[4,8,16,128]{3,2,1,0:T(8,128)(2,1)S(1)} collective-permute-done((bf16[4,8,16,128]{3,2,1,0:T(8,128)(2,1)S(1)}, bf16[4,8,16,128]{3,2,1,0:T(8,128)(2,1)S(1)}, u32[]{:S(2)}, u32[]{:S(2)}) %collective-permute-start) | collective-permute-done | bytes 131104 | tf_op jit(solution)/shard_map/ppermute | solution.py:261
  9.9 0.0 collective-permute-done.1.from_within
  9.9 0.0 copy-start
  9.9 0.0 copy-start.1
  9.9 0.0 copy-start.2
  9.9 0.6 %shard_map.114 = (bf16[8,16,128]{2,1,0:T(8,128)(2,1)S(1)}, f32[8,128]{1,0:T(8,128)S(1)}) custom-call(s32[8,24]{1,0:T(8,128)S(4)} %get-tuple-element.30.crossing, s32[8]{0:T(128)S(4)} %get-tuple-element.32.live, f32[8,128]{1,0:T(8,128)S(1)} %get-tuple-element.33.rows, bf16[4,8,16,128]{3,2,1,0:T(8,128)(2,1)S(1)} %get-tuple-element.34.across, ...), custom_call_target="tpu_custom_call" | custom-call | flops 100663296 | bytes 6291456 | tf_op jit(solution)/shard_map/pallas_call | solution.py:342
  10.5 2.1 %collective-permute-start.3 = (f32[8,128]{1,0:T(8,128)S(1)}, f32[8,128]{1,0:T(8,128)S(1)}, u32[]{:S(2)}, u32[]{:S(2)}) collective-permute-start(f32[8,128]{1,0:T(8,128)S(1)} %get-tuple-element.47), channel_id=1, source_target_pairs={{0,2},{1,3},{2,0},{3,1},{4,6},{5,7},{6,4},{7,5},{8,10},{9,11},{10,... | collective-permute-start | bytes 12296 | tf_op jit(solution)/shard_map/ppermute | solution.py:277
  12.6 0.0 copy-done.3
  12.6 0.7 %shard_map.115 = (f32[8,8,16,128]{3,2,1,0:T(8,128)S(1)}, bf16[4,8,16,128]{3,2,1,0:T(8,128)(2,1)S(1)}, bf16[4,8,16,128]{3,2,1,0:T(8,128)(2,1)S(1)}) custom-call(s32[8,24]{1,0:T(8,128)S(4)} %get-tuple-element.30.crossing, s32[128]{0:T(128)S(4)} %get-tuple-element.31.classes, s32[8]{0:T(128)S(4)} %get-tuple-element.32.live, f32[8,128]{1,0:T(8,128)S(1)} %copy-done.3, ...), custom_call_target="tpu_custom_call" | custom-call | flops 100663296 | bytes 6291456 | tf_op jit(solution)/shard_map/pallas_call | solution.py:353
  13.4 0.8 %collective-permute-done.3 = f32[8,128]{1,0:T(8,128)S(1)} collective-permute-done((f32[8,128]{1,0:T(8,128)S(1)}, f32[8,128]{1,0:T(8,128)S(1)}, u32[]{:S(2)}, u32[]{:S(2)}) %collective-permute-start.3) | collective-permute-done | bytes 4128 | tf_op jit(solution)/shard_map/ppermute | solution.py:277
  14.2 2.8 %collective-permute-start.4 = (f32[8,128]{1,0:T(8,128)S(1)}, f32[8,128]{1,0:T(8,128)S(1)}, u32[]{:S(2)}, u32[]{:S(2)}) collective-permute-start(f32[8,128]{1,0:T(8,128)S(1)} %add.6), channel_id=1, source_target_pairs={{0,8},{1,9},{2,10},{3,11},{4,12},{5,13},{6,14},{7,15},{8,0},{9,1},... | collective-permute-start | bytes 12296 | tf_op jit(solution)/shard_map/ppermute | solution.py:277
  17.0 0.9 %collective-permute-start.2 = (bf16[4,8,16,128]{3,2,1,0:T(8,128)(2,1)S(1)}, bf16[4,8,16,128]{3,2,1,0:T(8,128)(2,1)S(1)}, u32[]{:S(2)}, u32[]{:S(2)}) collective-permute-start(bf16[4,8,16,128]{3,2,1,0:T(8,128)(2,1)S(1)} %get-tuple-element.43), channel_id=1, source_target_pairs={{0,15},{1,2},{2,1},{3,4},{4,3},{5,6},{6,5},{7,8},{8,7},{9,10},{10,... | collective-permute-start | bytes 393224 | tf_op jit(solution)/shard_map/ppermute | solution.py:261
  17.9 0.8 %collective-permute-done.4 = f32[8,128]{1,0:T(8,128)S(1)} collective-permute-done((f32[8,128]{1,0:T(8,128)S(1)}, f32[8,128]{1,0:T(8,128)S(1)}, u32[]{:S(2)}, u32[]{:S(2)}) %collective-permute-start.4) | collective-permute-done | bytes 4128 | tf_op jit(solution)/shard_map/ppermute | solution.py:277
  18.7 0.9 %collective-permute-start.5 = (bf16[4,8,16,128]{3,2,1,0:T(8,128)(2,1)S(1)}, bf16[4,8,16,128]{3,2,1,0:T(8,128)(2,1)S(1)}, u32[]{:S(2)}, u32[]{:S(2)}) collective-permute-start(bf16[4,8,16,128]{3,2,1,0:T(8,128)(2,1)S(1)} %get-tuple-element.49), channel_id=1, source_target_pairs={{0,1},{1,0},{2,3},{3,2},{4,5},{5,4},{6,7},{7,6},{8,9},{9,8},{10,11... | collective-permute-start | bytes 393224 | tf_op jit(solution)/shard_map/ppermute | solution.py:265
  19.6 0.0 collective-permute-start.6
  19.6 0.3 %collective-permute-start.7 = (f32[8,128]{1,0:T(8,128)S(1)}, f32[8,128]{1,0:T(8,128)S(1)}, u32[]{:S(2)}, u32[]{:S(2)}) collective-permute-start(f32[8,128]{1,0:T(8,128)S(1)} %add.7.rest_0_), channel_id=1, source_target_pairs={{0,4},{1,5},{2,6},{3,7},{4,0},{5,1},{6,2},{7,3},{8,12},{9,13},{10,... | collective-permute-start | bytes 12296 | tf_op jit(solution)/shard_map/ppermute | solution.py:277
  19.9 1.5 %collective-permute-start.8 = (f32[8,128]{1,0:T(8,128)S(1)}, f32[8,128]{1,0:T(8,128)S(1)}, u32[]{:S(2)}, u32[]{:S(2)}) collective-permute-start(f32[8,128]{1,0:T(8,128)S(1)} %add.7.rest_0_), channel_id=1, source_target_pairs={{0,5},{1,4},{2,7},{3,6},{4,1},{5,0},{6,3},{7,2},{8,13},{9,12},{10,... | collective-permute-start | bytes 12296 | tf_op jit(solution)/shard_map/ppermute | solution.py:277
  21.4 0.0 collective-permute-done.6.rest_1_
  21.4 1.7 %collective-permute-done.7.rest_2_ = f32[8,128]{1,0:T(8,128)S(1)} collective-permute-done((f32[8,128]{1,0:T(8,128)S(1)}, f32[8,128]{1,0:T(8,128)S(1)}, u32[]{:S(2)}, u32[]{:S(2)}) %collective-permute-start.7) | collective-permute-done | bytes 4128 | tf_op jit(solution)/shard_map/ppermute | solution.py:277
  23.2 0.0 collective-permute-done.8.rest_3_
  23.2 0.9 %collective-permute-done.2.from_across = bf16[4,8,16,128]{3,2,1,0:T(8,128)(2,1)S(1)} collective-permute-done((bf16[4,8,16,128]{3,2,1,0:T(8,128)(2,1)S(1)}, bf16[4,8,16,128]{3,2,1,0:T(8,128)(2,1)S(1)}, u32[]{:S(2)}, u32[]{:S(2)}) %collective-permute-start.2) | collective-permute-done | bytes 131104 | tf_op jit(solution)/shard_map/ppermute | solution.py:261
  24.1 0.0 collective-permute-done.5.from_within
  24.1 0.0 copy-done
  24.1 0.0 copy-done.1
  24.1 0.0 copy-done.2
  24.1 1.2 %shard_map.116 = (f32[8,8,16,128]{3,2,1,0:T(8,128)}, f32[8,8,16,128]{3,2,1,0:T(8,128)}, f32[1,16]{1,0:T(1,128)}) custom-call(f32[8,8,16,128]{3,2,1,0:T(8,128)S(1)} %copy-done.2, f32[8,8,16,128]{3,2,1,0:T(8,128)S(1)} %copy-done.1, f32[8,8,16,128]{3,2,1,0:T(8,128)S(1)} %copy-done, f32[8,8,16,128]{3,2,1,0:T(8,128)S(1)} %get-tuple-element.42.image, ...), custom_call_target="tpu_custom_call" | custom-call | flops 1048576 | bytes 3670016 | tf_op jit(solution)/shard_map/pallas_call | solution.py:374
  (2 shorter events, 0.0 us)
Async XLA Ops:
  1.7 8.2 %collective-permute-start = (bf16[4,8,16,128]{3,2,1,0:T(8,128)(2,1)S(1)}, bf16[4,8,16,128]{3,2,1,0:T(8,128)(2,1)S(1)}, u32[]{:S(2)}, u32[]{:S(2)}) collective-permute-start(bf16[4,8,16,128]{3,2,1,0:T(8,128)(2,1)S(1)} %get-tuple-element.34.across), channel_id=1, source_target_pairs={{0,15},{1,2},{2,1},{3,4},{4,3},{5,6},{6,5},{7,8},{8,7},{9,10},{10,... | collective-permute-start | bytes 393224 | tf_op jit(solution)/shard_map/ppermute | solution.py:261
  7.2 2.7 %collective-permute-start.1 = (bf16[4,8,16,128]{3,2,1,0:T(8,128)(2,1)S(1)}, bf16[4,8,16,128]{3,2,1,0:T(8,128)(2,1)S(1)}, u32[]{:S(2)}, u32[]{:S(2)}) collective-permute-start(bf16[4,8,16,128]{3,2,1,0:T(8,128)(2,1)S(1)} %get-tuple-element.35.within), channel_id=1, source_target_pairs={{0,1},{1,0},{2,3},{3,2},{4,5},{5,4},{6,7},{7,6},{8,9},{9,8},{10,11... | collective-permute-start | bytes 393224 | tf_op jit(solution)/shard_map/ppermute | solution.py:265
  7.9 4.8 %copy-start.3 = (f32[8,128]{1,0:T(8,128)S(1)}, f32[8,128]{1,0:T(8,128)}, u32[]{:S(2)}) copy-start(f32[8,128]{1,0:T(8,128)} %smooth.1) | copy-start | bytes 12292
  9.9 14.2 %copy-start = (f32[8,8,16,128]{3,2,1,0:T(8,128)S(1)}, f32[8,8,16,128]{3,2,1,0:T(8,128)}, u32[]{:S(2)}) copy-start(f32[8,8,16,128]{3,2,1,0:T(8,128)} %direction.1) | copy-start | bytes 1572868
  9.9 14.2 %copy-start.1 = (f32[8,8,16,128]{3,2,1,0:T(8,128)S(1)}, f32[8,8,16,128]{3,2,1,0:T(8,128)}, u32[]{:S(2)}) copy-start(f32[8,8,16,128]{3,2,1,0:T(8,128)} %residual.1) | copy-start | bytes 1572868
  9.9 14.3 %copy-start.2 = (f32[8,8,16,128]{3,2,1,0:T(8,128)S(1)}, f32[8,8,16,128]{3,2,1,0:T(8,128)}, u32[]{:S(2)}) copy-start(f32[8,8,16,128]{3,2,1,0:T(8,128)} %solution.1) | copy-start | bytes 1572868
  10.5 3.7 %collective-permute-start.3 = (f32[8,128]{1,0:T(8,128)S(1)}, f32[8,128]{1,0:T(8,128)S(1)}, u32[]{:S(2)}, u32[]{:S(2)}) collective-permute-start(f32[8,128]{1,0:T(8,128)S(1)} %get-tuple-element.47), channel_id=1, source_target_pairs={{0,2},{1,3},{2,0},{3,1},{4,6},{5,7},{6,4},{7,5},{8,10},{9,11},{10,... | collective-permute-start | bytes 12296 | tf_op jit(solution)/shard_map/ppermute | solution.py:277
  14.2 4.5 %collective-permute-start.4 = (f32[8,128]{1,0:T(8,128)S(1)}, f32[8,128]{1,0:T(8,128)S(1)}, u32[]{:S(2)}, u32[]{:S(2)}) collective-permute-start(f32[8,128]{1,0:T(8,128)S(1)} %add.6), channel_id=1, source_target_pairs={{0,8},{1,9},{2,10},{3,11},{4,12},{5,13},{6,14},{7,15},{8,0},{9,1},... | collective-permute-start | bytes 12296 | tf_op jit(solution)/shard_map/ppermute | solution.py:277
  17.0 7.1 %collective-permute-start.2 = (bf16[4,8,16,128]{3,2,1,0:T(8,128)(2,1)S(1)}, bf16[4,8,16,128]{3,2,1,0:T(8,128)(2,1)S(1)}, u32[]{:S(2)}, u32[]{:S(2)}) collective-permute-start(bf16[4,8,16,128]{3,2,1,0:T(8,128)(2,1)S(1)} %get-tuple-element.43), channel_id=1, source_target_pairs={{0,15},{1,2},{2,1},{3,4},{4,3},{5,6},{6,5},{7,8},{8,7},{9,10},{10,... | collective-permute-start | bytes 393224 | tf_op jit(solution)/shard_map/ppermute | solution.py:261
  18.7 5.4 %collective-permute-start.5 = (bf16[4,8,16,128]{3,2,1,0:T(8,128)(2,1)S(1)}, bf16[4,8,16,128]{3,2,1,0:T(8,128)(2,1)S(1)}, u32[]{:S(2)}, u32[]{:S(2)}) collective-permute-start(bf16[4,8,16,128]{3,2,1,0:T(8,128)(2,1)S(1)} %get-tuple-element.49), channel_id=1, source_target_pairs={{0,1},{1,0},{2,3},{3,2},{4,5},{5,4},{6,7},{7,6},{8,9},{9,8},{10,11... | collective-permute-start | bytes 393224 | tf_op jit(solution)/shard_map/ppermute | solution.py:265
  19.6 1.9 %collective-permute-start.6 = (f32[8,128]{1,0:T(8,128)S(1)}, f32[8,128]{1,0:T(8,128)S(1)}, u32[]{:S(2)}, u32[]{:S(2)}) collective-permute-start(f32[8,128]{1,0:T(8,128)S(1)} %add.7.rest_0_), channel_id=1, source_target_pairs={{0,1},{1,0},{2,3},{3,2},{4,5},{5,4},{6,7},{7,6},{8,9},{9,8},{10,11... | collective-permute-start | bytes 12296 | tf_op jit(solution)/shard_map/ppermute | solution.py:277
  19.6 3.6 %collective-permute-start.7 = (f32[8,128]{1,0:T(8,128)S(1)}, f32[8,128]{1,0:T(8,128)S(1)}, u32[]{:S(2)}, u32[]{:S(2)}) collective-permute-start(f32[8,128]{1,0:T(8,128)S(1)} %add.7.rest_0_), channel_id=1, source_target_pairs={{0,4},{1,5},{2,6},{3,7},{4,0},{5,1},{6,2},{7,3},{8,12},{9,13},{10,... | collective-permute-start | bytes 12296 | tf_op jit(solution)/shard_map/ppermute | solution.py:277
  19.9 3.3 %collective-permute-start.8 = (f32[8,128]{1,0:T(8,128)S(1)}, f32[8,128]{1,0:T(8,128)S(1)}, u32[]{:S(2)}, u32[]{:S(2)}) collective-permute-start(f32[8,128]{1,0:T(8,128)S(1)} %add.7.rest_0_), channel_id=1, source_target_pairs={{0,5},{1,4},{2,7},{3,6},{4,1},{5,0},{6,3},{7,2},{8,13},{9,12},{10,... | collective-permute-start | bytes 12296 | tf_op jit(solution)/shard_map/ppermute | solution.py:277
